TPU v7x, 32 devices: a whole 2x2x4 slice. The times are simulated.
32 devices in a mesh: grp: 2 (over y), seq: 4 (over z), wt: 2 (over x), head: 2 (over core).
Axes of the slice: x: 2, y: 2, z: 4, core: 2. Of those that a mesh axis runs over, the one named last changes fastest.
Arguments:
- hidden: bfloat16 [2048, 2048], P(('grp', 'seq', 'wt'), 'head'), parts along dimension 0, may hold values from -6 to 6
- norm_gain: float32 [2048], replicated, may hold values from 0.1 to 1.9
- w_proj_x: bfloat16 [2048, 4096], P('wt', 'head'), may hold values from -0.125 to 0.125
- w_proj_bc: bfloat16 [2048, 512], P('wt', 'head'), may hold values from -0.125 to 0.125
- w_proj_dt: bfloat16 [2048, 32], P('wt', 'head'), may hold values from -0.125 to 0.125
- dt_bias: float32 [32], P('head'), may hold values from -4 to -1
- a_log: float32 [32], P('head'), may hold values from -20 to 1
- d_skip: float32 [32], P('head'), may hold values from 0.5 to 1.5
- inner_gain: float32 [4096], P('head'), may hold values from 0.1 to 1.9
- w_out: bfloat16 [4096, 2048], P('head', 'wt'), may hold values from -0.09375 to 0.09375
- lengths: int32 [16], P(('grp', 'seq', 'wt')), parts along dimension 0, may hold values from 1 to 128, 768 in all
- mix_index: int32 [16, 4], P(('grp', 'seq', 'wt')), parts along dimension 0, may hold values from 0 to 7, as said below
- mix_gain: float32 [16, 4], P(('grp', 'seq', 'wt')), parts along dimension 0, may hold values from -0.5 to 0.5
Outputs:
- layer_out: bfloat16 [2048, 2048], P(('grp', 'seq', 'wt'), 'head'), parts along dimension 0
There are 2 independent parts, one for each index of `grp`. A program takes and returns all parts, laid end to end along the dimension named above; an argument that names none is the same for every part. Nothing has to cross between parts.
Inputs may be any that keep to these rules, and one draw needn't show every extreme that they name: `mix_index`: each listed block belongs to the same shard of 128 positions as its row's block or to one of the two shards next to it.
All inputs are finite; a program needn't handle non-finite values. No bound on the sum of `lengths` on one device may be relied on, other than what follows from the above.
Results may differ from a plain program's by a relative error of at most 0.0065.
Values may be sent and summed in bfloat16 or wider, within the bound.
A program may use at most 320 MiB of HBM per device.

v0:
```python
import jax
import jax.numpy as jnp
from jax import lax
from jax.sharding import PartitionSpec as P

SPAN = 128
BLK = 128


eps_value = 1e-05
highest = lax.Precision.HIGHEST


def prefix(value, axis, join, neutral):
    count, mine = (lax.axis_size(axis), lax.axis_index(axis))
    pieces = jax.tree.map(lambda part: lax.all_gather(part, axis), value)
    total = jax.tree.map(
        lambda part, zero: jnp.full_like(part, 0) + jnp.asarray(zero, part.dtype), value, neutral
    )

    def turn(position, total):
        longer = join(total, jax.tree.map(lambda part: part[position], pieces))
        return jax.tree.map(lambda new, old: jnp.where(position < mine, new, old), longer, total)

    return lax.fori_loop(0, count - 1, turn, total)


def extended(cells, sides, width):
    for axis, dim in sides:
        count = lax.axis_size(axis)
        ends = count - 1
        head = lax.slice_in_dim(cells, 0, width, axis=dim)
        tail = lax.slice_in_dim(cells, cells.shape[dim] - width, cells.shape[dim], axis=dim)
        cells = jnp.concatenate(
            [
                lax.ppermute(tail, axis, [(i, (i + 1) % count) for i in range(ends)]),
                cells,
                lax.ppermute(head, axis, [((i + 1) % count, i) for i in range(ends)]),
            ],
            axis=dim,
        )
    return cells


def span_local(x_span, b_span, c_span, dt_span, log_span):
    cumulated = jnp.cumsum(log_span, axis=0)
    length = x_span.shape[0]
    rows_at = jnp.arange(length, dtype=jnp.int32)
    lower_part = rows_at[:, None] >= rows_at[None, :]
    difference = cumulated.T[:, :, None] - cumulated.T[:, None, :]
    decays = jnp.where(lower_part[None], jnp.exp(jnp.where(lower_part[None], difference, 0.0)), 0.0)
    scores = jnp.dot(c_span, b_span.T, precision=highest)
    weights = scores[None] * decays * dt_span.T[:, None, :]
    outputs = jnp.einsum("hts,shp->thp", weights, x_span, precision=highest)
    tail_decay = jnp.exp(cumulated[-1][None, :] - cumulated) * dt_span
    weighted_x = x_span * tail_decay[:, :, None]
    state_new = jnp.einsum("shp,sn->hpn", weighted_x, b_span, precision=highest)
    return (outputs, state_new, cumulated)


def from_state(c_span, cumulated, state_in):
    return (
        jnp.einsum("tn,hpn->thp", c_span, state_in, precision=highest)
        * jnp.exp(cumulated)[:, :, None]
    )


def combine(earlier, later):
    return (earlier[0] + later[0], jnp.exp(later[0])[:, None, None] * earlier[1] + later[1])


def body(
    hidden,
    norm_gain,
    w_proj_x,
    w_proj_bc,
    w_proj_dt,
    dt_bias,
    a_log,
    d_skip,
    inner_gain,
    w_out,
    lengths,
    mix_index,
    mix_gain,
):
    tokens_here = hidden.shape[0]
    half_width = hidden.shape[1]
    whole_input = lax.all_gather(hidden, "head", axis=1, tiled=True)
    floats = whole_input.astype(jnp.float32)
    normed = (
        floats
        * lax.rsqrt(jnp.mean(floats * floats, axis=-1, keepdims=True) + eps_value)
        * norm_gain
    ).astype(jnp.bfloat16)
    pieces = (
        lax.all_gather(w_proj_x, "wt", axis=0, tiled=True),
        lax.all_gather(w_proj_bc, "wt", axis=0, tiled=True),
        lax.all_gather(w_proj_dt, "wt", axis=0, tiled=True),
    )
    x_sum, bc_sum, dt_raw = tuple(
        (
            jnp.dot(normed, weight_piece, preferred_element_type=jnp.float32)
            for weight_piece in pieces
        )
    )
    heads_here = w_proj_dt.shape[1]
    state_size = w_proj_bc.shape[1] // 2
    head_size = w_proj_x.shape[1] // heads_here
    x_in = jax.nn.silu(x_sum).astype(jnp.bfloat16)
    bc_in = jax.nn.silu(bc_sum).astype(jnp.bfloat16)
    shard_at = lax.axis_index(("seq", "wt"))
    live_mask = (jnp.arange(tokens_here, dtype=jnp.int32) < lengths[0]).astype(jnp.float32)
    steps_dt = jax.nn.softplus(dt_raw + dt_bias) * live_mask[:, None]
    log_decay = -steps_dt * jnp.exp(a_log)
    spans = tokens_here // SPAN
    x_float = x_in.astype(jnp.float32).reshape(spans, SPAN, heads_here, head_size)
    b_float = bc_in[:, :state_size].astype(jnp.float32).reshape(spans, SPAN, state_size)
    c_float = bc_in[:, state_size:].astype(jnp.float32).reshape(spans, SPAN, state_size)
    dt_float = steps_dt.reshape(spans, SPAN, heads_here)
    log_float = log_decay.reshape(spans, SPAN, heads_here)
    outputs, fresh_states, cumulated = jax.vmap(span_local)(
        x_float, b_float, c_float, dt_float, log_float
    )
    running = jnp.zeros((heads_here, head_size, state_size), jnp.float32)
    before = jnp.zeros((heads_here,), jnp.float32)
    arriving = [running]
    decayed = [before]
    running = jnp.exp(cumulated[0, -1])[:, None, None] * running + fresh_states[0]
    before = cumulated[0, -1]
    identity_pair = (
        jnp.zeros((heads_here,), jnp.float32),
        jnp.zeros((heads_here, head_size, state_size), jnp.float32),
    )
    entering = prefix((before, running), ("seq", "wt"), combine, identity_pair)
    initial = entering[1]
    incoming = jnp.stack(arriving) + jnp.exp(jnp.stack(decayed))[:, :, None, None] * initial[None]
    outputs = outputs + jax.vmap(from_state)(c_float, cumulated, incoming)
    y_full = outputs.reshape(tokens_here, heads_here, head_size) + d_skip[
        None, :, None
    ] * x_float.reshape(tokens_here, heads_here, head_size)
    scaling = lax.rsqrt(jnp.mean(y_full * y_full, axis=-1, keepdims=True) + eps_value)
    y_norm = (
        (y_full * scaling * inner_gain.reshape(heads_here, head_size))
        .astype(jnp.bfloat16)
        .reshape(tokens_here, heads_here * head_size)
    )
    partial_out = jnp.dot(
        y_norm, lax.all_gather(w_out, "wt", axis=1, tiled=True), preferred_element_type=jnp.float32
    )
    head_total = lax.psum_scatter(partial_out, "head", scatter_dimension=1, tiled=True)
    own_part = hidden.astype(jnp.float32)
    mixed_in = (own_part + head_total).astype(jnp.bfloat16)
    widened = extended(mixed_in, ((("seq", "wt"), 0),), tokens_here)
    per_shard = tokens_here // BLK
    blocks = widened.reshape(3 * per_shard, BLK, half_width)
    relative = mix_index - (shard_at * per_shard - per_shard)
    summed_mix = mixed_in.astype(jnp.float32).reshape(per_shard, BLK, half_width)
    for member in range(mix_index.shape[1]):
        summed_mix = summed_mix + mix_gain[:, member][:, None, None] * jnp.take(
            blocks, relative[:, member], axis=0
        ).astype(jnp.float32)
    return summed_mix.reshape(tokens_here, half_width).astype(jnp.bfloat16)


def solution(mesh):
    in_specs = (
        P(("grp", "seq", "wt"), "head"),
        P(),
        P("wt", "head"),
        P("wt", "head"),
        P("wt", "head"),
        P("head"),
        P("head"),
        P("head"),
        P("head"),
        P("head", "wt"),
        P(("grp", "seq", "wt")),
        P(("grp", "seq", "wt"), None),
        P(("grp", "seq", "wt"), None),
    )
    out_specs = P(("grp", "seq", "wt"), "head")
    return jax.shard_map(body, mesh=mesh, in_specs=in_specs, out_specs=out_specs, check_vma=False)
```

profile of v0, /device:TPU:22, one launch (start us, length us, event | category | flops | bytes accessed | tf_op | source)
XLA Modules:
  0.0 415.9 jit_solution(728118675776157198)
XLA Ops:
  6.5 0.7 all-gather.9.cloned.1.call-update
  7.3 0.0 all-gather.7.cloned.1.call-start
  7.3 0.7 all-gather.7.cloned.1.call-update
  8.0 0.0 all-gather.13.cloned.1.call-start
  8.7 0.7 exp.58
  9.4 4.8 %all_gather.25 = bf16[2048,16]{0,1:T(8,128)(2,1)S(1)} all-gather(bf16[1024,16]{0,1:T(8,128)(2,1)} %param.21), channel_id=1, replica_groups=mesh['grp'=2,'seq'=4,'wt'=2,'head'=2] {'wt'}, dimensions={0}, use_global_device_ids=true | all-gather | bytes 98304 | tf_op jit(solution)/shard_map/all_gather | solution.py:99
  14.2 2.4 all_gather.22
  16.5 0.2 fusion.3
  16.7 1.0 fusion.39
  17.8 0.1 multiply_bitcast_fusion
  17.9 0.1 copy.23
  18.0 0.2 reduce_window_sum.13
  18.1 0.1 copy.27
  18.2 0.1 bitcast_exponential_fusion
  18.3 0.1 copy.28
  18.4 11.9 %all-gather.9.cloned.1.call-done = bf16[2048,256]{1,0:T(8,128)(2,1)} async-done(((bf16[1024,256]{1,0:T(8,128)(2,1)}), bf16[2048,256]{1,0:T(8,128)(2,1)}) %all-gather.9.cloned.1.call-update) | async-done | bytes 1048592 | tf_op jit(solution)/shard_map/all_gather | solution.py:98
  30.3 1.6 multiply_convert_fusion.1
  32.0 104.0 %all-gather.7.cloned.1.call-done = bf16[2048,2048]{1,0:T(8,128)(2,1)} async-done(((bf16[1024,2048]{1,0:T(8,128)(2,1)}), bf16[2048,2048]{1,0:T(8,128)(2,1)}) %all-gather.7.cloned.1.call-update) | async-done | bytes 8388624 | tf_op jit(solution)/shard_map/all_gather | solution.py:97
  135.9 0.3 mul.233
  136.3 5.3 %bitcast_multiply_fusion.1 = (f32[128,2048]{1,0:T(8,128)S(1)}, bf16[128,2048]{1,0:T(8,128)(2,1)S(1)}) fusion(f32[16,8,16,128]{3,2,1,0:T(8,128)S(1)} %bitcast.107, bf16[2048,2048]{1,0:T(8,128)(2,1)} %all-gather.7.cloned.1.call-done, bf16[128,2048]{1,0:T(8,128)(2,1)S(1)} %all_gather.22, f32[2048]{0:T(1024)S(1)} %copy-done.4, f32[128]{0:T(128)S(1)} %add_rsqrt_fusion.1), kind=kOutput, calls=%fused_computation.17 | convolution fusion | flops 1076625408 | bytes 11543040 | tf_op jit(solution)/shard_map/dot_general | solution.py:103
  141.5 0.0 copy-start.3
  141.5 0.3 copy.34
  141.9 1.6 convolution_add_fusion
  143.5 0.0 all-gather.13.cloned.1.call-update
  143.5 0.0 all-gather.11.cloned.1.call-start
  143.5 0.5 all-gather.11.cloned.1.call-update
  144.1 0.0 reduce-scatter.2.cloned.1.call-start
  144.1 0.1 copy.24
  144.2 14.2 %all-gather = f32[8,1,16]{2,1,0:T(1,128)S(1)} all-gather(f32[1,1,16]{2,1,0:T(1,128)S(1)} %get-tuple-element.141), channel_id=2, replica_groups=mesh['grp'=2,'seq'=4,'wt'=2,'head'=2] {'seq','wt'}, dimensions={0}, use_global_device_ids=true | all-gather | bytes 576 | tf_op jit(solution)/shard_map/all_gather | solution.py:16
  158.4 0.1 broadcast_bitcast_fusion
  158.5 0.1 fusion.35
  158.6 0.2 copy.36
  158.8 0.3 copy.33
  159.1 108.6 %all-gather.13.cloned.1.call-done = f32[128,128,128]{2,1,0:T(8,128)} async-done(((f32[16,128,128]{2,1,0:T(8,128)}), f32[128,128,128]{2,1,0:T(8,128)}) %all-gather.13.cloned.1.call-update) | async-done | bytes 8388624 | tf_op jit(solution)/shard_map/all_gather | solution.py:16
  267.7 10.8 %while.15 = (s32[]{:T(128)}, f32[16,128,128]{2,1,0:T(8,128)S(1)}, s32[]{:T(128)}, f32[8,16]{1,0:T(8,128)S(1)}, f32[8,16,128,128]{3,2,1,0:T(8,128)}, /*index=5*/s32[]{:T(128)}, s32[]{:T(128)}) while((s32[]{:T(128)}, f32[16,128,128]{2,1,0:T(8,128)S(1)}, s32[]{:T(128)}, f32[8,16]{1,0:T(8,128)S(1)}, f32[8,16,128,128]{3,2,1,0:T(8,128)}, ...), condition=%wide.region_3.4_spmd.clone, body=%wide.region_2.3_spmd.clone.sunk | while | flops 1048580 | bytes 3146025 | solution.py:25
  267.7 1.5 fusion.62
  269.2 1.5 fusion.62
  270.7 1.5 fusion.62
  272.2 1.5 fusion.62
  273.7 1.5 fusion.62
  275.2 1.6 fusion.62
  276.9 1.6 fusion.62
  278.5 0.0 copy-start.1
  278.5 0.6 fusion.1
  279.1 2.6 fusion.9
  281.7 0.1 copy.32
  281.8 1.7 copy.35
  283.5 88.7 %all-gather.11.cloned.1.call-done = bf16[2048,2048]{1,0:T(8,128)(2,1)} async-done(((bf16[2048,1024]{1,0:T(8,128)(2,1)}), bf16[2048,2048]{1,0:T(8,128)(2,1)}) %all-gather.11.cloned.1.call-update) | async-done | bytes 8388624 | tf_op jit(solution)/shard_map/all_gather | solution.py:149
  372.2 0.3 mul.247
  372.6 0.0 copy-start
  372.6 0.0 copy-start.5
  372.6 0.0 copy-start.2
  372.6 6.1 %fusion.16 = f32[128,2048]{1,0:T(8,128)} fusion(bf16[2048,2048]{1,0:T(8,128)(2,1)} %all-gather.11.cloned.1.call-done, f32[16,8,16,128]{3,2,1,0:T(8,128)S(1)} %bitcast.101, f32[128,2048]{1,0:T(8,128)S(1)} %copy.35, f32[2048]{0:T(1024)S(1)} %copy-done.1, f32[2048]{0:T(1024)S(1)} %broadcast_bitcast_fusion, bf16[128,2048]{1,0:T(8,128)(2,1)S(1)} %get-tuple-element.153), kind=kOutput, calls=%fused_computation.29 | convolution fusion | flops 1075314688 | bytes 12075008 | tf_op jit(solution)/shard_map/dot_general | solution.py:148
  378.7 0.0 reduce-scatter.2.cloned.1.call-update
  378.7 9.8 %reduce-scatter.2.cloned.1.call-done = f32[128,1024]{1,0:T(8,128)} async-done(((f32[128,2048]{1,0:T(8,128)}), f32[128,1024]{1,0:T(8,128)}) %reduce-scatter.2.cloned.1.call-update) | async-done | bytes 524304 | tf_op jit(solution)/shard_map/reduce_scatter | solution.py:151
  388.6 1.1 add_convert_fusion
  389.7 3.4 collective-permute-start
  393.1 2.4 collective-permute-start.1
  395.5 0.6 fusion.53
  403.6 0.7 fusion.52
  404.3 1.5 collective-permute-done
  405.7 0.0 collective-permute-done.1
  405.7 0.1 pad_maximum_fusion
  405.8 3.6 fusion.31
  (23 shorter events, 0.1 us)
Async XLA Ops:
  6.5 129.7 %copy-start.4 = (f32[2048]{0:T(1024)S(1)}, f32[2048]{0:T(1024)}, u32[]{:S(2)}) copy-start(f32[2048]{0:T(1024)} %param.18) | copy-start | bytes 24580
  6.5 23.8 %all-gather.9.cloned.1.call-start = ((), (), s32[]{:S(2)}) async-start(), calls=%async_computation.2 | async-start | bytes 1572864 | tf_op jit(solution)/shard_map/all_gather | solution.py:98
  7.3 128.7 %all-gather.7.cloned.1.call-start = ((), (), s32[]{:S(2)}) async-start(), calls=%async_computation.1 | async-start | bytes 12582912 | tf_op jit(solution)/shard_map/all_gather | solution.py:97
  8.0 259.7 %all-gather.13.cloned.1.call-start = ((), (), s32[]{:S(2)}) async-start(), calls=%async_computation.5 | async-start | bytes 9437184 | tf_op jit(solution)/shard_map/all_gather | solution.py:16
  141.5 16.9 %copy-start.3 = (f32[16]{0:T(128)S(1)}, f32[16]{0:T(128)}, u32[]{:S(2)}) copy-start(f32[16]{0:T(128)} %param.24) | copy-start | bytes 196
  143.5 228.7 %all-gather.11.cloned.1.call-start = ((), (), s32[]{:S(2)}) async-start(), calls=%async_computation.3 | async-start | bytes 12582912 | tf_op jit(solution)/shard_map/all_gather | solution.py:149
  144.1 244.5 %reduce-scatter.2.cloned.1.call-start = ((), (), s32[]{:S(2)}) async-start(), calls=%async_computation.4 | async-start | bytes 1572864 | tf_op jit(solution)/shard_map/reduce_scatter | solution.py:151
  278.5 94.1 %copy-start.1 = (f32[2048]{0:T(1024)S(1)}, f32[2048]{0:T(1024)}, u32[]{:S(2)}) copy-start(f32[2048]{0:T(1024)} %param.25) | copy-start | bytes 24580
  372.6 16.0 %copy-start = (bf16[128,1024]{1,0:T(8,128)(2,1)S(1)}, bf16[128,1024]{1,0:T(8,128)(2,1)}, u32[]{:S(2)}) copy-start(bf16[128,1024]{1,0:T(8,128)(2,1)} %param.17) | copy-start | bytes 786436
  372.6 22.9 %copy-start.5 = (s32[1,4]{1,0:T(1,128)S(1)}, s32[1,4]{1,0:T(1,128)}, u32[]{:S(2)}) copy-start(s32[1,4]{1,0:T(1,128)} %param.28) | copy-start | bytes 52
  372.6 31.0 %copy-start.2 = (f32[1,4]{1,0:T(1,128)S(1)}, f32[1,4]{1,0:T(1,128)}, u32[]{:S(2)}) copy-start(f32[1,4]{1,0:T(1,128)} %param.29) | copy-start | bytes 52
  389.7 16.1 %collective-permute-start = (bf16[128,1024]{1,0:T(8,128)(2,1)S(1)}, bf16[128,1024]{1,0:T(8,128)(2,1)S(1)}, u32[]{:S(2)}, u32[]{:S(2)}) collective-permute-start(bf16[128,1024]{1,0:T(8,128)(2,1)S(1)} %add_convert_fusion), channel_id=1, source_target_pairs={{0,2},{2,4},{4,6},{6,8},{8,10},{10,12},{12,14},{1,3},{3,5},{5,7},{... | collective-permute-start | bytes 786440 | tf_op jit(solution)/shard_map/ppermute | solution.py:36
  393.1 12.7 %collective-permute-start.1 = (bf16[128,1024]{1,0:T(8,128)(2,1)S(1)}, bf16[128,1024]{1,0:T(8,128)(2,1)S(1)}, u32[]{:S(2)}, u32[]{:S(2)}) collective-permute-start(bf16[128,1024]{1,0:T(8,128)(2,1)S(1)} %add_convert_fusion), channel_id=1, source_target_pairs={{2,0},{4,2},{6,4},{8,6},{10,8},{12,10},{14,12},{3,1},{5,3},{7,5},{... | collective-permute-start | bytes 786440 | tf_op jit(solution)/shard_map/ppermute | solution.py:38
Sparse Core Ops, SparseCore 0:
  8.9 21.3 all-gather.8
  31.9 103.9 all-gather.6
  143.6 124.0 all-gather.12
  269.1 103.0 all-gather.10
  378.8 9.6 reduce-scatter.1
where the time goes:
time: 418 us; the launch traced here: 416 us
  waiting for transfers between devices  326 us (78%)
  between operations  21.4 us (5%)
  blocking collectives  21.3 us (5%)
  matrix products  18.9 us (5%)
  other arithmetic  15.8 us (4%)
  starting transfers between devices  6 us (1%)
  local copies, waits for them, and re-layouts  5.71 us (1%)
    all_gather x1, waiting for transfers between devices, prefix(): pieces = jax.tree.map(lambda part: lax.all_gather(part, axis), value)  109 us
    all_gather x1, waiting for transfers between devices, body(): lax.all_gather(w_proj_x, 'wt', axis=0, tiled=True)  104 us
    all_gather x1, waiting for transfers between devices, body(): lax.all_gather(w_out, 'wt', axis=1, tiled=True)  88.7 us
    all_gather x1, blocking collectives, prefix(): pieces = jax.tree.map(lambda part: lax.all_gather(part, axis), value)  14.2 us
    all_gather x1, waiting for transfers between devices, body(): lax.all_gather(w_proj_bc, 'wt', axis=0, tiled=True)  11.9 us
    select_n x7, other arithmetic, turn(): jnp.where(position < mine, new, old)  10.5 us
    reduce_scatter x1, waiting for transfers between devices, body(): lax.psum_scatter(partial_out, 'head', scatter_dimension=1, tiled=True)  9.84 us
  transfers between devices with their start and end apart: 7, of which 6 were waited for; matrix products, arithmetic and copies ran while one was open for 5% of the time, Pallas kernels for 0%

commit v1 on v0

v1 whole, which is shorter than its diff:
```python
import jax
import jax.numpy as jnp
from jax import lax
from jax.sharding import PartitionSpec as P

EPS = 1e-05
BF = jnp.bfloat16
F32 = jnp.float32


def rotated(pick, axis):
    n, me = lax.axis_size(axis), lax.axis_index(axis)
    got = [pick(me)]
    for k in range(1, n):
        got.append(lax.ppermute(pick((me + k) % n), axis, [(i, (i + k) % n) for i in range(n)]))
    return got


def returned(parts, axis):
    n = lax.axis_size(axis)
    return [parts[0]] + [
        lax.ppermute(parts[k], axis, [(i, (i - k) % n) for i in range(n)]) for k in range(1, n)
    ]


def dot(a, b):
    return jnp.dot(a, b, preferred_element_type=F32)


def body(hidden, norm_gain, w_x, w_bc, w_dt, dt_bias, a_log, d_skip, inner_gain, w_out,
         lengths, mix_index, mix_gain):
    tokens, half = hidden.shape
    width = norm_gain.shape[0]
    depth = w_x.shape[0]
    heads = w_dt.shape[1]
    size = w_x.shape[1] // heads
    state = w_bc.shape[1] // 2
    n_wt, me_wt, me_head = lax.axis_size("wt"), lax.axis_index("wt"), lax.axis_index("head")
    floats = hidden.astype(F32)
    whole = lax.all_gather(hidden, "head", axis=1, tiled=True)
    wf = whole.astype(F32)
    scale = lax.rsqrt(jnp.mean(wf * wf, axis=-1, keepdims=True) + EPS)
    normed = (wf * scale * norm_gain).astype(BF)
    rows = jnp.concatenate(
        rotated(lambda j: lax.dynamic_slice_in_dim(normed, j * depth, depth, axis=1), "wt"), axis=0
    )
    px, pb, pd = dot(rows, w_x).reshape(n_wt, tokens, -1), dot(rows, w_bc), dot(rows, w_dt)
    ps = jnp.concatenate([pb, pd], axis=1).reshape(n_wt, tokens, -1)
    x_parts = returned([px[0]] + [px[k].astype(BF) for k in range(1, n_wt)], "wt")
    s_parts = returned([ps[k] for k in range(n_wt)], "wt")
    x_sum = sum(p.astype(F32) for p in x_parts)
    s_sum = sum(s_parts)
    x_in = jax.nn.silu(x_sum).astype(BF)
    bc = jax.nn.silu(s_sum[:, : 2 * state]).astype(BF)
    b, c = bc[:, :state], bc[:, state:]
    live = (jnp.arange(tokens, dtype=jnp.int32) < lengths[0]).astype(F32)
    dt = jax.nn.softplus(s_sum[:, 2 * state:] + dt_bias) * live[:, None]
    log = -dt * jnp.exp(a_log)
    at = jnp.arange(tokens)
    lower = at[:, None] >= at[None, :]
    cum = jnp.dot(lower.astype(F32), log, precision=lax.Precision.HIGHEST)
    shards = lax.all_gather(cum[-1], ("seq", "wt"))
    xh = x_in.reshape(tokens, heads, size)
    diff = cum.T[:, :, None] - cum.T[:, None, :]
    decay = jnp.exp(jnp.where(lower[None], diff, -jnp.inf))
    scores = dot(c, b.T)
    weights = (scores[None] * decay * dt.T[:, None, :]).astype(BF)
    local = jnp.einsum("hts,shp->thp", weights, xh, preferred_element_type=F32)
    tail = jnp.exp(cum[-1][None, :] - cum) * dt
    fresh = jnp.einsum(
        "sn,shp->nhp", b, (xh.astype(F32) * tail[:, :, None]).astype(BF), preferred_element_type=F32
    )
    count = lax.axis_size(("seq", "wt"))
    me = lax.axis_index(("seq", "wt"))
    order = jnp.arange(count)
    total = fresh
    entering = lax.ppermute(fresh.astype(BF), ("seq", "wt"), [(i, i + 1) for i in range(count - 1)])
    entering = entering.astype(F32)
    span = 1
    while span < count - 1:
        decay_sum = jnp.sum(jnp.where(((order >= me - span) & (order < me))[:, None], shards, 0.0), axis=0)
        came = lax.ppermute(
            entering.astype(BF), ("seq", "wt"), [(i, i + span) for i in range(count - span)]
        )
        entering = entering + jnp.exp(decay_sum)[None, :, None] * came.astype(F32)
        span *= 2
    y = local + jnp.exp(cum)[:, :, None] * jnp.einsum(
        "tn,nhp->thp", c, entering.astype(BF), preferred_element_type=F32
    )
    y = y + d_skip[None, :, None] * xh.astype(F32)
    scaling = lax.rsqrt(jnp.mean(y * y, axis=-1, keepdims=True) + EPS)
    y_norm = (y * scaling * inner_gain.reshape(heads, size)).astype(BF).reshape(tokens, heads * size)
    y_rows = jnp.concatenate(rotated(lambda j: y_norm, "wt"), axis=0)
    po = dot(y_rows, w_out).astype(BF).reshape(n_wt, tokens, -1)
    o_parts = returned([po[k] for k in range(n_wt)], "wt")
    cols = w_out.shape[1]
    partial = jnp.zeros((tokens, width), BF)
    for k, part in enumerate(o_parts):
        partial = lax.dynamic_update_slice_in_dim(partial, part, ((me_wt + k) % n_wt) * cols, axis=1)
    keep = lax.dynamic_slice_in_dim(partial, me_head * half, half, axis=1)
    give = lax.dynamic_slice_in_dim(partial, (1 - me_head) * half, half, axis=1)
    other = lax.ppermute(give, "head", [(0, 1), (1, 0)])
    mixed = (floats + keep.astype(F32) + other.astype(F32)).astype(BF)
    prev = lax.ppermute(mixed, ("seq", "wt"), [(i, i + 1) for i in range(count - 1)])
    nxt = lax.ppermute(mixed, ("seq", "wt"), [(i + 1, i) for i in range(count - 1)])
    rel = mix_index[0] - me
    gain = [jnp.sum(jnp.where(rel == j, mix_gain[0], 0.0)) for j in (-1, 0, 1)]
    out = mixed.astype(F32) * (1.0 + gain[1]) + gain[0] * prev.astype(F32) + gain[2] * nxt.astype(F32)
    return out.astype(BF)


def solution(mesh):
    in_specs = (
        P(("grp", "seq", "wt"), "head"), P(), P("wt", "head"), P("wt", "head"), P("wt", "head"),
        P("head"), P("head"), P("head"), P("head"), P("head", "wt"),
        P(("grp", "seq", "wt")), P(("grp", "seq", "wt"), None), P(("grp", "seq", "wt"), None),
    )
    return jax.shard_map(
        body, mesh=mesh, in_specs=in_specs, out_specs=P(("grp", "seq", "wt"), "head"), check_vma=False
    )
```

time: 418 us -> 145 us (0.35)
  the two profiles are of different devices: /device:TPU:22 before, /device:TPU:25 now
where the time goes in v1:
time: 145 us
  waiting for transfers between devices  86.4 us (60%)
  starting transfers between devices  22.9 us (16%)
  blocking collectives  18.9 us (13%)
  matrix products  6.96 us (5%)
  other arithmetic  6.35 us (4%)
  local copies, waits for them, and re-layouts  1.77 us (1%)
  between operations  1.73 us (1%)
    ppermute x3, waiting for transfers between devices, body(): lax.ppermute(entering.astype(BF), ('seq', 'wt'), [(i, i + span) for i in...  33 us
    ppermute x3, waiting for transfers between devices, returned(): lax.ppermute(parts[k], axis, [(i, (i - k) % n) for i in range(n)])  17.3 us
    all_gather x1, blocking collectives, body(): shards = lax.all_gather(cum[-1], ('seq', 'wt'))  16.1 us
    ppermute x2, waiting for transfers between devices, rotated(): lax.ppermute(pick((me + k) % n), axis, [(i, (i + k) % n) for i in range(n)])  14.7 us
    ppermute x1, waiting for transfers between devices, body(): lax.ppermute(fresh.astype(BF), ('seq', 'wt'), [(i, i + 1) for i in range(...  11.2 us
    ppermute x1, waiting for transfers between devices, body(): lax.ppermute(mixed, ('seq', 'wt'), [(i + 1, i) for i in range(count - 1)])  6.28 us
    ppermute x1, starting transfers between devices, body(): other = lax.ppermute(give, 'head', [(0, 1), (1, 0)])  5.81 us
    dot_general x5, matrix products, dot(): return jnp.dot(a, b, preferred_element_type=F32)  5.5 us
  transfers between devices with their start and end apart: 12, of which 11 were waited for; matrix products, arithmetic and copies ran while one was open for 2% of the time, Pallas kernels for 0%

profile of v1, /device:TPU:25, one launch (start us, length us, event | category | flops | bytes accessed | tf_op | source)
XLA Modules:
  0.0 145.1 jit_solution(12146311345958315747)
XLA Ops:
  0.0 0.0 copy-start
  0.0 2.8 %all_gather.6 = bf16[128,2048]{1,0:T(8,128)(2,1)S(1)} all-gather(bf16[128,1024]{1,0:T(8,128)(2,1)} %param.13), channel_id=1, replica_groups=mesh['grp'=2,'seq'=4,'wt'=2,'head'=2] {'head'}, dimensions={1}, use_global_device_ids=true | all-gather | bytes 786432 | tf_op jit(solution)/shard_map/all_gather | solution.py:40
  2.8 0.2 fusion.2
  3.0 0.0 copy-start.6
  3.0 1.0 fusion.4
  4.1 1.3 collective-permute-start
  6.1 0.7 exp.48
  6.7 5.0 %collective-permute-done = bf16[128,1024]{1,0:T(8,128)(2,1)S(1)} collective-permute-done((bf16[128,1024]{1,0:T(8,128)(2,1)S(1)}, bf16[128,1024]{1,0:T(8,128)(2,1)S(1)}, u32[]{:S(2)}, u32[]{:S(2)}) %collective-permute-start) | collective-permute-done | bytes 262176 | tf_op jit(solution)/shard_map/ppermute | solution.py:15
  11.7 0.0 copy-done
  11.7 0.3 fusion.20
  12.1 0.0 copy-done.7
  12.1 0.2 fusion.19
  12.3 0.0 copy-start.3
  12.4 1.3 collective-permute-start.2
  13.6 0.0 copy-done.6
  13.6 1.3 fusion.21
  14.9 0.1 slice.98
  15.0 0.3 collective-permute-start.1
  15.3 1.0 collective-permute-done.2
  16.4 0.2 fusion.31
  16.5 0.2 slice_reduce_fusion
  16.8 0.1 fusion.44
  16.9 11.1 %collective-permute-done.1 = bf16[128,2048]{1,0:T(8,128)(2,1)S(1)} collective-permute-done((bf16[128,2048]{1,0:T(8,128)(2,1)S(1)}, bf16[128,2048]{1,0:T(8,128)(2,1)S(1)}, u32[]{:S(2)}, u32[]{:S(2)}) %collective-permute-start.1) | collective-permute-done | bytes 524320 | tf_op jit(solution)/shard_map/ppermute | solution.py:22
  28.0 0.3 multiply_convert_fusion.2
  28.4 0.3 copy.31
  28.6 0.3 convolution_convert_fusion
  29.0 3.1 %collective-permute-start.3 = (bf16[128,16,128]{2,0,1:T(8,128)(2,1)S(1)}, bf16[128,16,128]{2,0,1:T(8,128)(2,1)S(1)}, u32[]{:S(2)}, u32[]{:S(2)}) collective-permute-start(bf16[128,16,128]{2,0,1:T(8,128)(2,1)S(1)} %convolution_convert_fusion), channel_id=1, source_target_pairs={{0,2},{2,4},{4,6},{6,8},{8,10},{10,12},{12,14},{1,3},{3,5},{5,7},{... | collective-permute-start | bytes 1572872 | tf_op jit(solution)/shard_map/ppermute | solution.py:77
  32.1 11.2 %collective-permute-done.3 = bf16[128,16,128]{2,0,1:T(8,128)(2,1)S(1)} collective-permute-done((bf16[128,16,128]{2,0,1:T(8,128)(2,1)S(1)}, bf16[128,16,128]{2,0,1:T(8,128)(2,1)S(1)}, u32[]{:S(2)}, u32[]{:S(2)}) %collective-permute-start.3) | collective-permute-done | bytes 524320 | tf_op jit(solution)/shard_map/ppermute | solution.py:77
  43.3 2.2 %collective-permute-start.4 = (bf16[128,16,128]{2,0,1:T(8,128)(2,1)S(1)}, bf16[128,16,128]{2,0,1:T(8,128)(2,1)S(1)}, u32[]{:S(2)}, u32[]{:S(2)}) collective-permute-start(bf16[128,16,128]{2,0,1:T(8,128)(2,1)S(1)} %collective-permute-done.3), channel_id=1, source_target_pairs={{0,2},{2,4},{4,6},{6,8},{8,10},{10,12},{12,14},{1,3},{3,5},{5,7},{... | collective-permute-start | bytes 1572872 | tf_op jit(solution)/shard_map/ppermute | solution.py:82
  45.6 16.1 %all-gather = f32[8,1,16]{2,1,0:T(1,128)S(1)} all-gather(f32[1,1,16]{2,1,0:T(1,128)S(1)} %bitcast.36), channel_id=1, replica_groups=mesh['grp'=2,'seq'=4,'wt'=2,'head'=2] {'seq','wt'}, dimensions={0}, use_global_device_ids=true | all-gather | bytes 576 | tf_op jit(solution)/shard_map/all_gather | solution.py:62
  61.6 0.1 select_reduce_fusion
  61.7 0.0 copy-start.8
  61.7 0.0 collective-permute-done.4
  61.7 0.2 fusion.9
  62.0 1.3 collective-permute-start.5
  63.3 8.6 %collective-permute-done.5 = bf16[128,16,128]{2,0,1:T(8,128)(2,1)S(1)} collective-permute-done((bf16[128,16,128]{2,0,1:T(8,128)(2,1)S(1)}, bf16[128,16,128]{2,0,1:T(8,128)(2,1)S(1)}, u32[]{:S(2)}, u32[]{:S(2)}) %collective-permute-start.5) | collective-permute-done | bytes 524320 | tf_op jit(solution)/shard_map/ppermute | solution.py:82
  71.9 0.4 fusion.10
  72.4 1.3 collective-permute-start.6
  73.7 0.2 fusion.26
  73.9 0.0 copy-start.2
  73.9 24.4 %collective-permute-done.6 = bf16[128,16,128]{2,0,1:T(8,128)(2,1)S(1)} collective-permute-done((bf16[128,16,128]{2,0,1:T(8,128)(2,1)S(1)}, bf16[128,16,128]{2,0,1:T(8,128)(2,1)S(1)}, u32[]{:S(2)}, u32[]{:S(2)}) %collective-permute-start.6) | collective-permute-done | bytes 524320 | tf_op jit(solution)/shard_map/ppermute | solution.py:82
  98.3 0.5 add_convert_fusion
  98.8 0.3 copy.28
  99.1 0.3 fusion.28
  99.4 0.7 multiply_reduce_fusion
  100.1 0.3 multiply_convert_fusion
  100.5 0.1 collective-permute-start.7
  100.5 0.0 copy-start.1
  100.6 0.0 copy-start.4
  100.6 0.0 copy-start.5
  100.6 9.7 %collective-permute-done.7 = bf16[128,2048]{0,1:T(8,128)(2,1)S(1)} collective-permute-done((bf16[128,2048]{0,1:T(8,128)(2,1)S(1)}, bf16[128,2048]{0,1:T(8,128)(2,1)S(1)}, u32[]{:S(2)}, u32[]{:S(2)}) %collective-permute-start.7) | collective-permute-done | bytes 524320 | tf_op jit(solution)/shard_map/ppermute | solution.py:15
  110.3 3.5 %convolution_convert_fusion.1 = bf16[256,1024]{1,0:T(8,128)(2,1)S(1)} fusion(bf16[2048,1024]{1,0:T(8,128)(2,1)} %param.22, bf16[128,2048]{0,1:T(8,128)(2,1)S(1)} %collective-permute-done.7, bf16[128,2048]{0,1:T(8,128)(2,1)S(1)} %bitcast.32), kind=kOutput, calls=%fused_computation.8 | convolution fusion | flops 1076101120 | bytes 5767168 | tf_op jit(solution)/shard_map/dot_general | solution.py:27
  113.8 0.1 collective-permute-start.8
  113.9 5.2 %collective-permute-done.8 = bf16[128,1024]{1,0:T(8,128)(2,1)S(1)} collective-permute-done((bf16[128,1024]{1,0:T(8,128)(2,1)S(1)}, bf16[128,1024]{1,0:T(8,128)(2,1)S(1)}, u32[]{:S(2)}, u32[]{:S(2)}) %collective-permute-start.8) | collective-permute-done | bytes 262176 | tf_op jit(solution)/shard_map/ppermute | solution.py:22
  119.2 5.8 %collective-permute-start.9 = (bf16[128,1024]{1,0:T(8,128)(2,1)S(1)}, bf16[128,1024]{1,0:T(8,128)(2,1)S(1)}, u32[]{:S(2)}, u32[]{:S(2)}) collective-permute-start(bf16[128,1024]{1,0:T(8,128)(2,1)S(1)} %constant_dynamic-slice_fusion), channel_id=1, source_target_pairs={{0,1},{1,0},{2,3},{3,2},{4,5},{5,4},{6,7},{7,6},{8,9},{9,8},{10,11... | collective-permute-start | bytes 786440 | tf_op jit(solution)/shard_map/ppermute | solution.py:102
  125.0 1.2 collective-permute-done.9
  126.2 0.0 copy-done.1
  126.2 0.1 add_convert_fusion.2
  126.3 2.1 %collective-permute-start.10 = (bf16[128,1024]{1,0:T(8,128)(2,1)S(1)}, bf16[128,1024]{1,0:T(8,128)(2,1)S(1)}, u32[]{:S(2)}, u32[]{:S(2)}) collective-permute-start(bf16[128,1024]{1,0:T(8,128)(2,1)S(1)} %add_convert_fusion.2), channel_id=1, source_target_pairs={{0,2},{2,4},{4,6},{6,8},{8,10},{10,12},{12,14},{1,3},{3,5},{5,7},{... | collective-permute-start | bytes 786440 | tf_op jit(solution)/shard_map/ppermute | solution.py:104
  128.4 4.1 %collective-permute-start.11 = (bf16[128,1024]{1,0:T(8,128)(2,1)S(1)}, bf16[128,1024]{1,0:T(8,128)(2,1)S(1)}, u32[]{:S(2)}, u32[]{:S(2)}) collective-permute-start(bf16[128,1024]{1,0:T(8,128)(2,1)S(1)} %add_convert_fusion.2), channel_id=1, source_target_pairs={{2,0},{4,2},{6,4},{8,6},{10,8},{12,10},{14,12},{3,1},{5,3},{7,5},{... | collective-permute-start | bytes 786440 | tf_op jit(solution)/shard_map/ppermute | solution.py:105
  132.5 0.7 fusion.36
  133.8 2.8 %collective-permute-done.10 = bf16[128,1024]{1,0:T(8,128)(2,1)S(1)} collective-permute-done((bf16[128,1024]{1,0:T(8,128)(2,1)S(1)}, bf16[128,1024]{1,0:T(8,128)(2,1)S(1)}, u32[]{:S(2)}, u32[]{:S(2)}) %collective-permute-start.10) | collective-permute-done | bytes 262176 | tf_op jit(solution)/shard_map/ppermute | solution.py:104
  136.7 6.3 %collective-permute-done.11 = bf16[128,1024]{1,0:T(8,128)(2,1)S(1)} collective-permute-done((bf16[128,1024]{1,0:T(8,128)(2,1)S(1)}, bf16[128,1024]{1,0:T(8,128)(2,1)S(1)}, u32[]{:S(2)}, u32[]{:S(2)}) %collective-permute-start.11) | collective-permute-done | bytes 262176 | tf_op jit(solution)/shard_map/ppermute | solution.py:105
  142.9 2.1 %add_convert_fusion.1 = bf16[128,1024]{1,0:T(8,128)(2,1)} fusion(bf16[128,1024]{1,0:T(8,128)(2,1)S(1)} %collective-permute-done.11, bf16[128,1024]{1,0:T(8,128)(2,1)S(1)} %collective-permute-done.10, bf16[128,1024]{1,0:T(8,128)(2,1)S(1)} %add_convert_fusion.2, f32[]{:T(128)} %get-tuple-element.9, f32[]{:T(128)} %get-tuple-element.10, f32[]{:T(128)S(6)} %add_shard_map.3), kind=kLoop, calls=%fused_computation.28 | loop fusion | flops 1179648 | bytes 1048588 | tf_op jit(solution)/shard_map/convert_element_type | solution.py:109
  (23 shorter events, 0.4 us)
Async XLA Ops:
  0.0 11.7 %copy-start = (bf16[1024,256]{1,0:T(8,128)(2,1)S(1)}, bf16[1024,256]{1,0:T(8,128)(2,1)}, u32[]{:S(2)}) copy-start(bf16[1024,256]{1,0:T(8,128)(2,1)} %param.16) | copy-start | bytes 1572868
  0.0 12.1 %copy-start.7 = (bf16[1024,16]{0,1:T(8,128)(2,1)S(1)}, bf16[1024,16]{0,1:T(8,128)(2,1)}, u32[]{:S(2)}) copy-start(bf16[1024,16]{0,1:T(8,128)(2,1)} %param.17) | copy-start | bytes 98308
  3.0 10.6 %copy-start.6 = (bf16[1024,2048]{1,0:T(8,128)(2,1)S(1)}, bf16[1024,2048]{1,0:T(8,128)(2,1)}, u32[]{:S(2)}) copy-start(bf16[1024,2048]{1,0:T(8,128)(2,1)} %param.15) | copy-start | bytes 12582916
  4.1 7.6 %collective-permute-start = (bf16[128,1024]{1,0:T(8,128)(2,1)S(1)}, bf16[128,1024]{1,0:T(8,128)(2,1)S(1)}, u32[]{:S(2)}, u32[]{:S(2)}) collective-permute-start(bf16[128,1024]{1,0:T(8,128)(2,1)S(1)} %get-tuple-element.14), channel_id=1, source_target_pairs={{0,2},{2,0},{1,3},{3,1},{4,6},{6,4},{5,7},{7,5},{8,10},{10,8},{9,1... | collective-permute-start | bytes 786440 | tf_op jit(solution)/shard_map/ppermute | solution.py:15
  12.3 4.0 %copy-start.3 = (f32[16]{0:T(128)S(1)}, f32[16]{0:T(128)}, u32[]{:S(2)}) copy-start(f32[16]{0:T(128)} %param.18) | copy-start | bytes 196
  12.4 4.0 %collective-permute-start.2 = (f32[128,272]{0,1:T(8,128)S(1)}, f32[128,272]{0,1:T(8,128)S(1)}, u32[]{:S(2)}, u32[]{:S(2)}) collective-permute-start(f32[128,272]{0,1:T(8,128)S(1)} %pad_maximum_fusion.4), channel_id=1, source_target_pairs={{0,2},{2,0},{1,3},{3,1},{4,6},{6,4},{5,7},{7,5},{8,10},{10,8},{9,1... | collective-permute-start | bytes 417800 | tf_op jit(solution)/shard_map/ppermute | solution.py:22
  15.0 13.0 %collective-permute-start.1 = (bf16[128,2048]{1,0:T(8,128)(2,1)S(1)}, bf16[128,2048]{1,0:T(8,128)(2,1)S(1)}, u32[]{:S(2)}, u32[]{:S(2)}) collective-permute-start(bf16[128,2048]{1,0:T(8,128)(2,1)S(1)} %slice.98), channel_id=1, source_target_pairs={{0,2},{2,0},{1,3},{3,1},{4,6},{6,4},{5,7},{7,5},{8,10},{10,8},{9,1... | collective-permute-start | bytes 1572872 | tf_op jit(solution)/shard_map/ppermute | solution.py:22
  29.0 14.3 %collective-permute-start.3 = (bf16[128,16,128]{2,0,1:T(8,128)(2,1)S(1)}, bf16[128,16,128]{2,0,1:T(8,128)(2,1)S(1)}, u32[]{:S(2)}, u32[]{:S(2)}) collective-permute-start(bf16[128,16,128]{2,0,1:T(8,128)(2,1)S(1)} %convolution_convert_fusion), channel_id=1, source_target_pairs={{0,2},{2,4},{4,6},{6,8},{8,10},{10,12},{12,14},{1,3},{3,5},{5,7},{... | collective-permute-start | bytes 1572872 | tf_op jit(solution)/shard_map/ppermute | solution.py:77
  43.3 18.4 %collective-permute-start.4 = (bf16[128,16,128]{2,0,1:T(8,128)(2,1)S(1)}, bf16[128,16,128]{2,0,1:T(8,128)(2,1)S(1)}, u32[]{:S(2)}, u32[]{:S(2)}) collective-permute-start(bf16[128,16,128]{2,0,1:T(8,128)(2,1)S(1)} %collective-permute-done.3), channel_id=1, source_target_pairs={{0,2},{2,4},{4,6},{6,8},{8,10},{10,12},{12,14},{1,3},{3,5},{5,7},{... | collective-permute-start | bytes 1572872 | tf_op jit(solution)/shard_map/ppermute | solution.py:82
  61.7 37.7 %copy-start.8 = (f32[16]{0:T(128)S(1)}, f32[16]{0:T(128)}, u32[]{:S(2)}) copy-start(f32[16]{0:T(128)} %param.20) | copy-start | bytes 196
  62.0 9.9 %collective-permute-start.5 = (bf16[128,16,128]{2,0,1:T(8,128)(2,1)S(1)}, bf16[128,16,128]{2,0,1:T(8,128)(2,1)S(1)}, u32[]{:S(2)}, u32[]{:S(2)}) collective-permute-start(bf16[128,16,128]{2,0,1:T(8,128)(2,1)S(1)} %fusion.9), channel_id=1, source_target_pairs={{0,4},{2,6},{4,8},{6,10},{8,12},{10,14},{1,5},{3,7},{5,9},{7,11},{... | collective-permute-start | bytes 1572872 | tf_op jit(solution)/shard_map/ppermute | solution.py:82
  72.4 25.9 %collective-permute-start.6 = (bf16[128,16,128]{2,0,1:T(8,128)(2,1)S(1)}, bf16[128,16,128]{2,0,1:T(8,128)(2,1)S(1)}, u32[]{:S(2)}, u32[]{:S(2)}) collective-permute-start(bf16[128,16,128]{2,0,1:T(8,128)(2,1)S(1)} %fusion.10), channel_id=1, source_target_pairs={{0,8},{2,10},{4,12},{6,14},{1,9},{3,11},{5,13},{7,15},{16,24},{18,... | collective-permute-start | bytes 1572872 | tf_op jit(solution)/shard_map/ppermute | solution.py:82
  73.9 26.2 %copy-start.2 = (f32[2048]{0:T(1024)S(1)}, f32[2048]{0:T(1024)}, u32[]{:S(2)}) copy-start(f32[2048]{0:T(1024)} %param.21) | copy-start | bytes 24580
  100.5 9.8 %collective-permute-start.7 = (bf16[128,2048]{0,1:T(8,128)(2,1)S(1)}, bf16[128,2048]{0,1:T(8,128)(2,1)S(1)}, u32[]{:S(2)}, u32[]{:S(2)}) collective-permute-start(bf16[128,2048]{0,1:T(8,128)(2,1)S(1)} %bitcast.31), channel_id=1, source_target_pairs={{0,2},{2,0},{1,3},{3,1},{4,6},{6,4},{5,7},{7,5},{8,10},{10,8},{9,1... | collective-permute-start | bytes 1572872 | tf_op jit(solution)/shard_map/ppermute | solution.py:15
  100.5 25.6 %copy-start.1 = (bf16[128,1024]{1,0:T(8,128)(2,1)S(1)}, bf16[128,1024]{1,0:T(8,128)(2,1)}, u32[]{:S(2)}) copy-start(bf16[128,1024]{1,0:T(8,128)(2,1)} %param.13) | copy-start | bytes 786436
  100.6 31.9 %copy-start.4 = (f32[1,4]{1,0:T(1,128)S(1)}, f32[1,4]{1,0:T(1,128)}, u32[]{:S(2)}) copy-start(f32[1,4]{1,0:T(1,128)} %param.25) | copy-start | bytes 52
  100.6 31.9 %copy-start.5 = (s32[1,4]{1,0:T(1,128)S(1)}, s32[1,4]{1,0:T(1,128)}, u32[]{:S(2)}) copy-start(s32[1,4]{1,0:T(1,128)} %param.24) | copy-start | bytes 52
  113.8 5.3 %collective-permute-start.8 = (bf16[128,1024]{1,0:T(8,128)(2,1)S(1)}, bf16[128,1024]{1,0:T(8,128)(2,1)S(1)}, u32[]{:S(2)}, u32[]{:S(2)}) collective-permute-start(bf16[128,1024]{1,0:T(8,128)(2,1)S(1)} %get-tuple-element.11), channel_id=1, source_target_pairs={{0,2},{2,0},{1,3},{3,1},{4,6},{6,4},{5,7},{7,5},{8,10},{10,8},{9,1... | collective-permute-start | bytes 786440 | tf_op jit(solution)/shard_map/ppermute | solution.py:22
  119.2 7.0 %collective-permute-start.9 = (bf16[128,1024]{1,0:T(8,128)(2,1)S(1)}, bf16[128,1024]{1,0:T(8,128)(2,1)S(1)}, u32[]{:S(2)}, u32[]{:S(2)}) collective-permute-start(bf16[128,1024]{1,0:T(8,128)(2,1)S(1)} %constant_dynamic-slice_fusion), channel_id=1, source_target_pairs={{0,1},{1,0},{2,3},{3,2},{4,5},{5,4},{6,7},{7,6},{8,9},{9,8},{10,11... | collective-permute-start | bytes 786440 | tf_op jit(solution)/shard_map/ppermute | solution.py:102
  126.3 10.4 %collective-permute-start.10 = (bf16[128,1024]{1,0:T(8,128)(2,1)S(1)}, bf16[128,1024]{1,0:T(8,128)(2,1)S(1)}, u32[]{:S(2)}, u32[]{:S(2)}) collective-permute-start(bf16[128,1024]{1,0:T(8,128)(2,1)S(1)} %add_convert_fusion.2), channel_id=1, source_target_pairs={{0,2},{2,4},{4,6},{6,8},{8,10},{10,12},{12,14},{1,3},{3,5},{5,7},{... | collective-permute-start | bytes 786440 | tf_op jit(solution)/shard_map/ppermute | solution.py:104
  128.4 14.5 %collective-permute-start.11 = (bf16[128,1024]{1,0:T(8,128)(2,1)S(1)}, bf16[128,1024]{1,0:T(8,128)(2,1)S(1)}, u32[]{:S(2)}, u32[]{:S(2)}) collective-permute-start(bf16[128,1024]{1,0:T(8,128)(2,1)S(1)} %add_convert_fusion.2), channel_id=1, source_target_pairs={{2,0},{4,2},{6,4},{8,6},{10,8},{12,10},{14,12},{3,1},{5,3},{7,5},{... | collective-permute-start | bytes 786440 | tf_op jit(solution)/shard_map/ppermute | solution.py:105

commit v2 on v1

--- a/solution.py
+++ b/solution.py
@@ -59,7 +59,6 @@
     at = jnp.arange(tokens)
     lower = at[:, None] >= at[None, :]
     cum = jnp.dot(lower.astype(F32), log, precision=lax.Precision.HIGHEST)
-    shards = lax.all_gather(cum[-1], ("seq", "wt"))
     xh = x_in.reshape(tokens, heads, size)
     diff = cum.T[:, :, None] - cum.T[:, None, :]
     decay = jnp.exp(jnp.where(lower[None], diff, -jnp.inf))
@@ -72,17 +71,17 @@
     )
     count = lax.axis_size(("seq", "wt"))
     me = lax.axis_index(("seq", "wt"))
-    order = jnp.arange(count)
-    total = fresh
+    decay_sum = lax.ppermute(cum[-1], ("seq", "wt"), [(i, i + 1) for i in range(count - 1)])
     entering = lax.ppermute(fresh.astype(BF), ("seq", "wt"), [(i, i + 1) for i in range(count - 1)])
     entering = entering.astype(F32)
     span = 1
     while span < count - 1:
-        decay_sum = jnp.sum(jnp.where(((order >= me - span) & (order < me))[:, None], shards, 0.0), axis=0)
+        decay_came = lax.ppermute(decay_sum, ("seq", "wt"), [(i, i + span) for i in range(count - span)])
         came = lax.ppermute(
             entering.astype(BF), ("seq", "wt"), [(i, i + span) for i in range(count - span)]
         )
         entering = entering + jnp.exp(decay_sum)[None, :, None] * came.astype(F32)
+        decay_sum = decay_sum + decay_came
         span *= 2
     y = local + jnp.exp(cum)[:, :, None] * jnp.einsum(
         "tn,nhp->thp", c, entering.astype(BF), preferred_element_type=F32

time: 145 us -> 147 us (1.014)
  the two profiles are of different devices: /device:TPU:25 before, /device:TPU:22 now
where the time goes in v2:
time: 147 us; the launch traced here: 144 us
  waiting for transfers between devices  89.5 us (61%)
  starting transfers between devices  35.9 us (24%)
  matrix products  6.99 us (5%)
  other arithmetic  6.13 us (4%)
  blocking collectives  2.51 us (2%)
  local copies, waits for them, and re-layouts  1.74 us (1%)
  between operations  1.68 us (1%)
    ppermute x2, waiting for transfers between devices, body(): lax.ppermute(decay_sum, ('seq', 'wt'), [(i, i + span) for i in range(coun...  19.1 us
    ppermute x2, waiting for transfers between devices, rotated(): lax.ppermute(pick((me + k) % n), axis, [(i, (i + k) % n) for i in range(n)])  17.6 us
    ppermute x3, waiting for transfers between devices, returned(): lax.ppermute(parts[k], axis, [(i, (i - k) % n) for i in range(n)])  17 us
    ppermute x1, waiting for transfers between devices, body(): lax.ppermute(fresh.astype(BF), ('seq', 'wt'), [(i, i + 1) for i in range(...  10.9 us
    ppermute x3, waiting for transfers between devices, body(): lax.ppermute(entering.astype(BF), ('seq', 'wt'), [(i, i + span) for i in...  8.87 us
    ppermute x3, starting transfers between devices, body(): lax.ppermute(entering.astype(BF), ('seq', 'wt'), [(i, i + span) for i in...  8.3 us
    ppermute x2, starting transfers between devices, body(): lax.ppermute(decay_sum, ('seq', 'wt'), [(i, i + span) for i in range(coun...  7.85 us
    ppermute x1, waiting for transfers between devices, body(): lax.ppermute(mixed, ('seq', 'wt'), [(i, i + 1) for i in range(count - 1)])  7.78 us
  transfers between devices with their start and end apart: 15, of which 12 were waited for; matrix products, arithmetic and copies ran while one was open for 2% of the time, Pallas kernels for 0%

profile of v2, /device:TPU:22, one launch (start us, length us, event | category | flops | bytes accessed | tf_op | source)
XLA Modules:
  0.0 144.4 jit_solution(13164074448440403987)
XLA Ops:
  0.0 0.0 copy-start
  0.0 2.5 %all_gather.3 = bf16[128,2048]{1,0:T(8,128)(2,1)S(1)} all-gather(bf16[128,1024]{1,0:T(8,128)(2,1)} %param.13), channel_id=1, replica_groups=mesh['grp'=2,'seq'=4,'wt'=2,'head'=2] {'head'}, dimensions={1}, use_global_device_ids=true | all-gather | bytes 786432 | tf_op jit(solution)/shard_map/all_gather | solution.py:40
  2.5 0.2 fusion.2
  2.7 0.0 copy-start.6
  2.7 1.0 fusion.4
  3.8 0.6 collective-permute-start
  5.1 0.7 exp.36
  5.7 6.5 %collective-permute-done = bf16[128,1024]{1,0:T(8,128)(2,1)S(1)} collective-permute-done((bf16[128,1024]{1,0:T(8,128)(2,1)S(1)}, bf16[128,1024]{1,0:T(8,128)(2,1)S(1)}, u32[]{:S(2)}, u32[]{:S(2)}) %collective-permute-start) | collective-permute-done | bytes 262176 | tf_op jit(solution)/shard_map/ppermute | solution.py:15
  12.2 0.0 copy-done
  12.2 0.3 fusion.20
  12.6 0.2 fusion.19
  12.9 0.0 copy-start.3
  12.9 0.6 collective-permute-start.2
  13.5 1.3 fusion.21
  14.8 0.1 slice.98
  14.8 1.6 %collective-permute-start.1 = (bf16[128,2048]{1,0:T(8,128)(2,1)S(1)}, bf16[128,2048]{1,0:T(8,128)(2,1)S(1)}, u32[]{:S(2)}, u32[]{:S(2)}) collective-permute-start(bf16[128,2048]{1,0:T(8,128)(2,1)S(1)} %slice.98), channel_id=1, source_target_pairs={{0,2},{2,0},{1,3},{3,1},{4,6},{6,4},{5,7},{7,5},{8,10},{10,8},{9,1... | collective-permute-start | bytes 1572872 | tf_op jit(solution)/shard_map/ppermute | solution.py:22
  16.4 3.1 %collective-permute-done.2 = f32[128,272]{0,1:T(8,128)S(1)} collective-permute-done((f32[128,272]{0,1:T(8,128)S(1)}, f32[128,272]{0,1:T(8,128)S(1)}, u32[]{:S(2)}, u32[]{:S(2)}) %collective-permute-start.2) | collective-permute-done | bytes 139296 | tf_op jit(solution)/shard_map/ppermute | solution.py:22
  19.5 0.0 copy-done.3
  19.5 0.2 fusion.31
  19.7 0.2 slice_reduce_fusion
  19.9 0.1 fusion.44
  20.1 9.2 %collective-permute-done.1 = bf16[128,2048]{1,0:T(8,128)(2,1)S(1)} collective-permute-done((bf16[128,2048]{1,0:T(8,128)(2,1)S(1)}, bf16[128,2048]{1,0:T(8,128)(2,1)S(1)}, u32[]{:S(2)}, u32[]{:S(2)}) %collective-permute-start.1) | collective-permute-done | bytes 524320 | tf_op jit(solution)/shard_map/ppermute | solution.py:22
  29.2 0.3 multiply_convert_fusion.2
  29.6 0.3 copy.26
  29.8 0.3 convolution_convert_fusion
  30.2 3.5 %collective-permute-start.3 = (bf16[128,16,128]{2,0,1:T(8,128)(2,1)S(1)}, bf16[128,16,128]{2,0,1:T(8,128)(2,1)S(1)}, u32[]{:S(2)}, u32[]{:S(2)}) collective-permute-start(bf16[128,16,128]{2,0,1:T(8,128)(2,1)S(1)} %convolution_convert_fusion), channel_id=1, source_target_pairs={{0,2},{2,4},{4,6},{6,8},{8,10},{10,12},{12,14},{1,3},{3,5},{5,7},{... | collective-permute-start | bytes 1572872 | tf_op jit(solution)/shard_map/ppermute | solution.py:75
  33.6 10.9 %collective-permute-done.3 = bf16[128,16,128]{2,0,1:T(8,128)(2,1)S(1)} collective-permute-done((bf16[128,16,128]{2,0,1:T(8,128)(2,1)S(1)}, bf16[128,16,128]{2,0,1:T(8,128)(2,1)S(1)}, u32[]{:S(2)}, u32[]{:S(2)}) %collective-permute-start.3) | collective-permute-done | bytes 524320 | tf_op jit(solution)/shard_map/ppermute | solution.py:75
  44.5 4.3 %collective-permute-start.5 = (bf16[128,16,128]{2,0,1:T(8,128)(2,1)S(1)}, bf16[128,16,128]{2,0,1:T(8,128)(2,1)S(1)}, u32[]{:S(2)}, u32[]{:S(2)}) collective-permute-start(bf16[128,16,128]{2,0,1:T(8,128)(2,1)S(1)} %collective-permute-done.3), channel_id=1, source_target_pairs={{0,2},{2,4},{4,6},{6,8},{8,10},{10,12},{12,14},{1,3},{3,5},{5,7},{... | collective-permute-start | bytes 1572872 | tf_op jit(solution)/shard_map/ppermute | solution.py:80
  48.8 2.5 %collective-permute-start.4 = (f32[16]{0:T(128)S(1)}, f32[16]{0:T(128)S(1)}, u32[]{:S(2)}, u32[]{:S(2)}) collective-permute-start(f32[16]{0:T(128)S(1)} %slice_reduce_fusion), channel_id=1, source_target_pairs={{0,2},{2,4},{4,6},{6,8},{8,10},{10,12},{12,14},{1,3},{3,5},{5,7},{... | collective-permute-start | bytes 200 | tf_op jit(solution)/shard_map/ppermute | solution.py:74
  51.4 6.7 %collective-permute-done.4 = f32[16]{0:T(128)S(1)} collective-permute-done((f32[16]{0:T(128)S(1)}, f32[16]{0:T(128)S(1)}, u32[]{:S(2)}, u32[]{:S(2)}) %collective-permute-start.4) | collective-permute-done | bytes 96 | tf_op jit(solution)/shard_map/ppermute | solution.py:74
  58.0 5.2 %collective-permute-start.6 = (f32[16]{0:T(128)S(1)}, f32[16]{0:T(128)S(1)}, u32[]{:S(2)}, u32[]{:S(2)}) collective-permute-start(f32[16]{0:T(128)S(1)} %collective-permute-done.4), channel_id=1, source_target_pairs={{0,2},{2,4},{4,6},{6,8},{8,10},{10,12},{12,14},{1,3},{3,5},{5,7},{... | collective-permute-start | bytes 200 | tf_op jit(solution)/shard_map/ppermute | solution.py:79
  63.2 1.3 collective-permute-done.6
  64.5 0.0 collective-permute-done.5
  64.5 0.0 copy-start.8
  64.5 0.2 fusion.9
  64.8 2.7 %collective-permute-start.7 = (bf16[128,16,128]{2,0,1:T(8,128)(2,1)S(1)}, bf16[128,16,128]{2,0,1:T(8,128)(2,1)S(1)}, u32[]{:S(2)}, u32[]{:S(2)}) collective-permute-start(bf16[128,16,128]{2,0,1:T(8,128)(2,1)S(1)} %fusion.9), channel_id=1, source_target_pairs={{0,4},{2,6},{4,8},{6,10},{8,12},{10,14},{1,5},{3,7},{5,9},{7,11},{... | collective-permute-start | bytes 1572872 | tf_op jit(solution)/shard_map/ppermute | solution.py:80
  67.5 8.9 %collective-permute-done.7 = bf16[128,16,128]{2,0,1:T(8,128)(2,1)S(1)} collective-permute-done((bf16[128,16,128]{2,0,1:T(8,128)(2,1)S(1)}, bf16[128,16,128]{2,0,1:T(8,128)(2,1)S(1)}, u32[]{:S(2)}, u32[]{:S(2)}) %collective-permute-start.7) | collective-permute-done | bytes 524320 | tf_op jit(solution)/shard_map/ppermute | solution.py:80
  76.3 0.4 fusion.10
  76.8 1.3 collective-permute-start.9
  78.1 2.7 %collective-permute-start.8 = (f32[16]{0:T(128)S(1)}, f32[16]{0:T(128)S(1)}, u32[]{:S(2)}, u32[]{:S(2)}) collective-permute-start(f32[16]{0:T(128)S(1)} %get-tuple-element.9), channel_id=1, source_target_pairs={{0,4},{2,6},{4,8},{6,10},{8,12},{10,14},{1,5},{3,7},{5,9},{7,11},{... | collective-permute-start | bytes 200 | tf_op jit(solution)/shard_map/ppermute | solution.py:79
  80.8 0.2 fusion.26
  81.0 17.9 %collective-permute-done.8 = f32[16]{0:T(128)S(1)} collective-permute-done((f32[16]{0:T(128)S(1)}, f32[16]{0:T(128)S(1)}, u32[]{:S(2)}, u32[]{:S(2)}) %collective-permute-start.8) | collective-permute-done | bytes 96 | tf_op jit(solution)/shard_map/ppermute | solution.py:79
  98.9 0.0 collective-permute-done.9
  98.9 0.5 add_convert_fusion
  99.4 0.3 copy.23
  99.7 0.3 fusion.28
  100.0 0.0 copy-done.8
  100.0 0.7 multiply_reduce_fusion
  100.7 0.0 copy-done.2
  100.7 0.3 multiply_convert_fusion
  101.1 2.4 %collective-permute-start.10 = (bf16[128,2048]{0,1:T(8,128)(2,1)S(1)}, bf16[128,2048]{0,1:T(8,128)(2,1)S(1)}, u32[]{:S(2)}, u32[]{:S(2)}) collective-permute-start(bf16[128,2048]{0,1:T(8,128)(2,1)S(1)} %bitcast.29), channel_id=1, source_target_pairs={{0,2},{2,0},{1,3},{3,1},{4,6},{6,4},{5,7},{7,5},{8,10},{10,8},{9,1... | collective-permute-start | bytes 1572872 | tf_op jit(solution)/shard_map/ppermute | solution.py:15
  103.4 11.1 %collective-permute-done.10 = bf16[128,2048]{0,1:T(8,128)(2,1)S(1)} collective-permute-done((bf16[128,2048]{0,1:T(8,128)(2,1)S(1)}, bf16[128,2048]{0,1:T(8,128)(2,1)S(1)}, u32[]{:S(2)}, u32[]{:S(2)}) %collective-permute-start.10) | collective-permute-done | bytes 524320 | tf_op jit(solution)/shard_map/ppermute | solution.py:15
  114.5 3.5 %convolution_convert_fusion.1 = bf16[256,1024]{1,0:T(8,128)(2,1)S(1)} fusion(bf16[2048,1024]{1,0:T(8,128)(2,1)} %param.22, bf16[128,2048]{0,1:T(8,128)(2,1)S(1)} %collective-permute-done.10, bf16[128,2048]{0,1:T(8,128)(2,1)S(1)} %bitcast.30), kind=kOutput, calls=%fused_computation.8 | convolution fusion | flops 1076101120 | bytes 5767168 | tf_op jit(solution)/shard_map/dot_general | solution.py:27
  118.1 1.8 %collective-permute-start.11 = (bf16[128,1024]{1,0:T(8,128)(2,1)S(1)}, bf16[128,1024]{1,0:T(8,128)(2,1)S(1)}, u32[]{:S(2)}, u32[]{:S(2)}) collective-permute-start(bf16[128,1024]{1,0:T(8,128)(2,1)S(1)} %get-tuple-element.10), channel_id=1, source_target_pairs={{0,2},{2,0},{1,3},{3,1},{4,6},{6,4},{5,7},{7,5},{8,10},{10,8},{9,1... | collective-permute-start | bytes 786440 | tf_op jit(solution)/shard_map/ppermute | solution.py:22
  119.9 4.8 %collective-permute-done.11 = bf16[128,1024]{1,0:T(8,128)(2,1)S(1)} collective-permute-done((bf16[128,1024]{1,0:T(8,128)(2,1)S(1)}, bf16[128,1024]{1,0:T(8,128)(2,1)S(1)}, u32[]{:S(2)}, u32[]{:S(2)}) %collective-permute-start.11) | collective-permute-done | bytes 262176 | tf_op jit(solution)/shard_map/ppermute | solution.py:22
  124.8 0.1 collective-permute-start.12
  124.8 1.5 %collective-permute-done.12 = bf16[128,1024]{1,0:T(8,128)(2,1)S(1)} collective-permute-done((bf16[128,1024]{1,0:T(8,128)(2,1)S(1)}, bf16[128,1024]{1,0:T(8,128)(2,1)S(1)}, u32[]{:S(2)}, u32[]{:S(2)}) %collective-permute-start.12) | collective-permute-done | bytes 262176 | tf_op jit(solution)/shard_map/ppermute | solution.py:101
  126.4 0.1 add_convert_fusion.2
  126.5 4.8 %collective-permute-start.13 = (bf16[128,1024]{1,0:T(8,128)(2,1)S(1)}, bf16[128,1024]{1,0:T(8,128)(2,1)S(1)}, u32[]{:S(2)}, u32[]{:S(2)}) collective-permute-start(bf16[128,1024]{1,0:T(8,128)(2,1)S(1)} %add_convert_fusion.2), channel_id=1, source_target_pairs={{0,2},{2,4},{4,6},{6,8},{8,10},{10,12},{12,14},{1,3},{3,5},{5,7},{... | collective-permute-start | bytes 786440 | tf_op jit(solution)/shard_map/ppermute | solution.py:103
  131.3 1.9 %collective-permute-start.14 = (bf16[128,1024]{1,0:T(8,128)(2,1)S(1)}, bf16[128,1024]{1,0:T(8,128)(2,1)S(1)}, u32[]{:S(2)}, u32[]{:S(2)}) collective-permute-start(bf16[128,1024]{1,0:T(8,128)(2,1)S(1)} %add_convert_fusion.2), channel_id=1, source_target_pairs={{2,0},{4,2},{6,4},{8,6},{10,8},{12,10},{14,12},{3,1},{5,3},{7,5},{... | collective-permute-start | bytes 786440 | tf_op jit(solution)/shard_map/ppermute | solution.py:104
  133.3 0.6 fusion.36
  134.6 7.8 %collective-permute-done.13 = bf16[128,1024]{1,0:T(8,128)(2,1)S(1)} collective-permute-done((bf16[128,1024]{1,0:T(8,128)(2,1)S(1)}, bf16[128,1024]{1,0:T(8,128)(2,1)S(1)}, u32[]{:S(2)}, u32[]{:S(2)}) %collective-permute-start.13) | collective-permute-done | bytes 262176 | tf_op jit(solution)/shard_map/ppermute | solution.py:103
  142.3 0.0 collective-permute-done.14
  142.3 2.0 %add_convert_fusion.1 = bf16[128,1024]{1,0:T(8,128)(2,1)} fusion(bf16[128,1024]{1,0:T(8,128)(2,1)S(1)} %collective-permute-done.14, bf16[128,1024]{1,0:T(8,128)(2,1)S(1)} %collective-permute-done.13, bf16[128,1024]{1,0:T(8,128)(2,1)S(1)} %add_convert_fusion.2, f32[]{:T(128)} %get-tuple-element.6, f32[]{:T(128)} %get-tuple-element.7, f32[]{:T(128)S(6)} %add_shard_map.3), kind=kLoop, calls=%fused_computation.28 | loop fusion | flops 1179648 | bytes 1048588 | tf_op jit(solution)/shard_map/convert_element_type | solution.py:108
  (24 shorter events, 0.3 us)
Async XLA Ops:
  0.0 12.2 %copy-start = (bf16[1024,256]{1,0:T(8,128)(2,1)S(1)}, bf16[1024,256]{1,0:T(8,128)(2,1)}, u32[]{:S(2)}) copy-start(bf16[1024,256]{1,0:T(8,128)(2,1)} %param.16) | copy-start | bytes 1572868
  0.0 12.6 %copy-start.7 = (bf16[1024,16]{0,1:T(8,128)(2,1)S(1)}, bf16[1024,16]{0,1:T(8,128)(2,1)}, u32[]{:S(2)}) copy-start(bf16[1024,16]{0,1:T(8,128)(2,1)} %param.17) | copy-start | bytes 98308
  2.7 10.8 %copy-start.6 = (bf16[1024,2048]{1,0:T(8,128)(2,1)S(1)}, bf16[1024,2048]{1,0:T(8,128)(2,1)}, u32[]{:S(2)}) copy-start(bf16[1024,2048]{1,0:T(8,128)(2,1)} %param.15) | copy-start | bytes 12582916
  3.8 8.4 %collective-permute-start = (bf16[128,1024]{1,0:T(8,128)(2,1)S(1)}, bf16[128,1024]{1,0:T(8,128)(2,1)S(1)}, u32[]{:S(2)}, u32[]{:S(2)}) collective-permute-start(bf16[128,1024]{1,0:T(8,128)(2,1)S(1)} %get-tuple-element.13), channel_id=1, source_target_pairs={{0,2},{2,0},{1,3},{3,1},{4,6},{6,4},{5,7},{7,5},{8,10},{10,8},{9,1... | collective-permute-start | bytes 786440 | tf_op jit(solution)/shard_map/ppermute | solution.py:15
  12.9 6.6 %copy-start.3 = (f32[16]{0:T(128)S(1)}, f32[16]{0:T(128)}, u32[]{:S(2)}) copy-start(f32[16]{0:T(128)} %param.18) | copy-start | bytes 196
  12.9 6.6 %collective-permute-start.2 = (f32[128,272]{0,1:T(8,128)S(1)}, f32[128,272]{0,1:T(8,128)S(1)}, u32[]{:S(2)}, u32[]{:S(2)}) collective-permute-start(f32[128,272]{0,1:T(8,128)S(1)} %pad_maximum_fusion.4), channel_id=1, source_target_pairs={{0,2},{2,0},{1,3},{3,1},{4,6},{6,4},{5,7},{7,5},{8,10},{10,8},{9,1... | collective-permute-start | bytes 417800 | tf_op jit(solution)/shard_map/ppermute | solution.py:22
  14.8 14.4 %collective-permute-start.1 = (bf16[128,2048]{1,0:T(8,128)(2,1)S(1)}, bf16[128,2048]{1,0:T(8,128)(2,1)S(1)}, u32[]{:S(2)}, u32[]{:S(2)}) collective-permute-start(bf16[128,2048]{1,0:T(8,128)(2,1)S(1)} %slice.98), channel_id=1, source_target_pairs={{0,2},{2,0},{1,3},{3,1},{4,6},{6,4},{5,7},{7,5},{8,10},{10,8},{9,1... | collective-permute-start | bytes 1572872 | tf_op jit(solution)/shard_map/ppermute | solution.py:22
  30.2 14.4 %collective-permute-start.3 = (bf16[128,16,128]{2,0,1:T(8,128)(2,1)S(1)}, bf16[128,16,128]{2,0,1:T(8,128)(2,1)S(1)}, u32[]{:S(2)}, u32[]{:S(2)}) collective-permute-start(bf16[128,16,128]{2,0,1:T(8,128)(2,1)S(1)} %convolution_convert_fusion), channel_id=1, source_target_pairs={{0,2},{2,4},{4,6},{6,8},{8,10},{10,12},{12,14},{1,3},{3,5},{5,7},{... | collective-permute-start | bytes 1572872 | tf_op jit(solution)/shard_map/ppermute | solution.py:75
  44.5 20.0 %collective-permute-start.5 = (bf16[128,16,128]{2,0,1:T(8,128)(2,1)S(1)}, bf16[128,16,128]{2,0,1:T(8,128)(2,1)S(1)}, u32[]{:S(2)}, u32[]{:S(2)}) collective-permute-start(bf16[128,16,128]{2,0,1:T(8,128)(2,1)S(1)} %collective-permute-done.3), channel_id=1, source_target_pairs={{0,2},{2,4},{4,6},{6,8},{8,10},{10,12},{12,14},{1,3},{3,5},{5,7},{... | collective-permute-start | bytes 1572872 | tf_op jit(solution)/shard_map/ppermute | solution.py:80
  48.8 9.2 %collective-permute-start.4 = (f32[16]{0:T(128)S(1)}, f32[16]{0:T(128)S(1)}, u32[]{:S(2)}, u32[]{:S(2)}) collective-permute-start(f32[16]{0:T(128)S(1)} %slice_reduce_fusion), channel_id=1, source_target_pairs={{0,2},{2,4},{4,6},{6,8},{8,10},{10,12},{12,14},{1,3},{3,5},{5,7},{... | collective-permute-start | bytes 200 | tf_op jit(solution)/shard_map/ppermute | solution.py:74
  58.0 6.4 %collective-permute-start.6 = (f32[16]{0:T(128)S(1)}, f32[16]{0:T(128)S(1)}, u32[]{:S(2)}, u32[]{:S(2)}) collective-permute-start(f32[16]{0:T(128)S(1)} %collective-permute-done.4), channel_id=1, source_target_pairs={{0,2},{2,4},{4,6},{6,8},{8,10},{10,12},{12,14},{1,3},{3,5},{5,7},{... | collective-permute-start | bytes 200 | tf_op jit(solution)/shard_map/ppermute | solution.py:79
  64.5 35.5 %copy-start.8 = (f32[16]{0:T(128)S(1)}, f32[16]{0:T(128)}, u32[]{:S(2)}) copy-start(f32[16]{0:T(128)} %param.20) | copy-start | bytes 196
  64.8 11.6 %collective-permute-start.7 = (bf16[128,16,128]{2,0,1:T(8,128)(2,1)S(1)}, bf16[128,16,128]{2,0,1:T(8,128)(2,1)S(1)}, u32[]{:S(2)}, u32[]{:S(2)}) collective-permute-start(bf16[128,16,128]{2,0,1:T(8,128)(2,1)S(1)} %fusion.9), channel_id=1, source_target_pairs={{0,4},{2,6},{4,8},{6,10},{8,12},{10,14},{1,5},{3,7},{5,9},{7,11},{... | collective-permute-start | bytes 1572872 | tf_op jit(solution)/shard_map/ppermute | solution.py:80
  76.8 22.1 %collective-permute-start.9 = (bf16[128,16,128]{2,0,1:T(8,128)(2,1)S(1)}, bf16[128,16,128]{2,0,1:T(8,128)(2,1)S(1)}, u32[]{:S(2)}, u32[]{:S(2)}) collective-permute-start(bf16[128,16,128]{2,0,1:T(8,128)(2,1)S(1)} %fusion.10), channel_id=1, source_target_pairs={{0,8},{2,10},{4,12},{6,14},{1,9},{3,11},{5,13},{7,15},{16,24},{18,... | collective-permute-start | bytes 1572872 | tf_op jit(solution)/shard_map/ppermute | solution.py:80
  78.1 20.7 %collective-permute-start.8 = (f32[16]{0:T(128)S(1)}, f32[16]{0:T(128)S(1)}, u32[]{:S(2)}, u32[]{:S(2)}) collective-permute-start(f32[16]{0:T(128)S(1)} %get-tuple-element.9), channel_id=1, source_target_pairs={{0,4},{2,6},{4,8},{6,10},{8,12},{10,14},{1,5},{3,7},{5,9},{7,11},{... | collective-permute-start | bytes 200 | tf_op jit(solution)/shard_map/ppermute | solution.py:79
  98.9 1.8 %copy-start.2 = (f32[2048]{0:T(1024)S(1)}, f32[2048]{0:T(1024)}, u32[]{:S(2)}) copy-start(f32[2048]{0:T(1024)} %param.21) | copy-start | bytes 24580
  101.1 13.4 %collective-permute-start.10 = (bf16[128,2048]{0,1:T(8,128)(2,1)S(1)}, bf16[128,2048]{0,1:T(8,128)(2,1)S(1)}, u32[]{:S(2)}, u32[]{:S(2)}) collective-permute-start(bf16[128,2048]{0,1:T(8,128)(2,1)S(1)} %bitcast.29), channel_id=1, source_target_pairs={{0,2},{2,0},{1,3},{3,1},{4,6},{6,4},{5,7},{7,5},{8,10},{10,8},{9,1... | collective-permute-start | bytes 1572872 | tf_op jit(solution)/shard_map/ppermute | solution.py:15
  103.4 22.9 %copy-start.1 = (bf16[128,1024]{1,0:T(8,128)(2,1)S(1)}, bf16[128,1024]{1,0:T(8,128)(2,1)}, u32[]{:S(2)}) copy-start(bf16[128,1024]{1,0:T(8,128)(2,1)} %param.13) | copy-start | bytes 786436
  103.4 29.8 %copy-start.4 = (f32[1,4]{1,0:T(1,128)S(1)}, f32[1,4]{1,0:T(1,128)}, u32[]{:S(2)}) copy-start(f32[1,4]{1,0:T(1,128)} %param.25) | copy-start | bytes 52
  103.4 29.9 %copy-start.5 = (s32[1,4]{1,0:T(1,128)S(1)}, s32[1,4]{1,0:T(1,128)}, u32[]{:S(2)}) copy-start(s32[1,4]{1,0:T(1,128)} %param.24) | copy-start | bytes 52
  118.1 6.6 %collective-permute-start.11 = (bf16[128,1024]{1,0:T(8,128)(2,1)S(1)}, bf16[128,1024]{1,0:T(8,128)(2,1)S(1)}, u32[]{:S(2)}, u32[]{:S(2)}) collective-permute-start(bf16[128,1024]{1,0:T(8,128)(2,1)S(1)} %get-tuple-element.10), channel_id=1, source_target_pairs={{0,2},{2,0},{1,3},{3,1},{4,6},{6,4},{5,7},{7,5},{8,10},{10,8},{9,1... | collective-permute-start | bytes 786440 | tf_op jit(solution)/shard_map/ppermute | solution.py:22
  124.8 1.6 %collective-permute-start.12 = (bf16[128,1024]{1,0:T(8,128)(2,1)S(1)}, bf16[128,1024]{1,0:T(8,128)(2,1)S(1)}, u32[]{:S(2)}, u32[]{:S(2)}) collective-permute-start(bf16[128,1024]{1,0:T(8,128)(2,1)S(1)} %constant_dynamic-slice_fusion), channel_id=1, source_target_pairs={{0,1},{1,0},{2,3},{3,2},{4,5},{5,4},{6,7},{7,6},{8,9},{9,8},{10,11... | collective-permute-start | bytes 786440 | tf_op jit(solution)/shard_map/ppermute | solution.py:101
  126.5 15.9 %collective-permute-start.13 = (bf16[128,1024]{1,0:T(8,128)(2,1)S(1)}, bf16[128,1024]{1,0:T(8,128)(2,1)S(1)}, u32[]{:S(2)}, u32[]{:S(2)}) collective-permute-start(bf16[128,1024]{1,0:T(8,128)(2,1)S(1)} %add_convert_fusion.2), channel_id=1, source_target_pairs={{0,2},{2,4},{4,6},{6,8},{8,10},{10,12},{12,14},{1,3},{3,5},{5,7},{... | collective-permute-start | bytes 786440 | tf_op jit(solution)/shard_map/ppermute | solution.py:103
  131.3 11.0 %collective-permute-start.14 = (bf16[128,1024]{1,0:T(8,128)(2,1)S(1)}, bf16[128,1024]{1,0:T(8,128)(2,1)S(1)}, u32[]{:S(2)}, u32[]{:S(2)}) collective-permute-start(bf16[128,1024]{1,0:T(8,128)(2,1)S(1)} %add_convert_fusion.2), channel_id=1, source_target_pairs={{2,0},{4,2},{6,4},{8,6},{10,8},{12,10},{14,12},{3,1},{5,3},{7,5},{... | collective-permute-start | bytes 786440 | tf_op jit(solution)/shard_map/ppermute | solution.py:104

commit v3 on v2

v3 whole, which is shorter than its diff:
```python
import functools

import jax
import jax.numpy as jnp
from jax import lax
from jax.experimental import pallas as pl
from jax.experimental.pallas import tpu as pltpu
from jax.sharding import PartitionSpec as P

EPS = 1e-05
BF = jnp.bfloat16
F32 = jnp.float32
MESH = pl.DeviceIdType.MESH
DMA = pltpu.SemaphoreType.DMA


def dot(a, b):
    return jnp.dot(a, b, preferred_element_type=F32)


def silu(v):
    return v * jax.nn.sigmoid(v)


def kernel(n_seq, n_wt, heads, hid, params, norm_gain, gains, wx_hbm, wbc, wdt, wo_hbm, out,
           hid_all, normed, rows, prod, small, wx, wo, x_in, cum_t, dt_t, fresh, e_in, e_out, yb,
           po, partial, hrec, mixed, prev_b, next_b,
           sem_w, sem_h, sem_r, sem_p, sem_s, sem_e, sem_y, sem_o, sem_g, sem_n):
    z, w, hd = lax.axis_index("seq"), lax.axis_index("wt"), lax.axis_index("head")
    tokens, half = hid.shape
    depth, cols = wx.shape[0], wo.shape[1]
    chan = wx.shape[1]
    count = n_seq * n_wt
    me = z * n_wt + w
    sib = {"head": 1 - hd}

    def peer(k):
        return {"wt": lax.rem(w + k + n_wt, n_wt)}

    def shard(step):
        at = lax.rem(me + step + count, count)
        return {"seq": at // n_wt, "wt": lax.rem(at, n_wt)}

    def remote(src, dst, sems, device):
        return pltpu.make_async_remote_copy(src_ref=src, dst_ref=dst, send_sem=sems.at[0],
                                            recv_sem=sems.at[1], device_id=device, device_id_type=MESH)

    load_x = pltpu.make_async_copy(wx_hbm, wx, sem_w.at[0])
    load_o = pltpu.make_async_copy(wo_hbm, wo, sem_w.at[1])
    load_x.start()
    load_o.start()
    barrier = pltpu.get_barrier_semaphore()
    for device in [sib, shard(1), shard(-1)] + [peer(k) for k in range(1, n_wt)]:
        pl.semaphore_signal(barrier, inc=1, device_id=device, device_id_type=MESH)
    pl.semaphore_wait(barrier, 3 + n_wt - 1)

    def block(at, size):
        return pl.ds(pl.multiple_of(at * size, 128), size)

    swap = remote(hid, hid_all.at[:, block(hd, half)], sem_h, sib)
    swap.start()
    hid_all[:, block(hd, half)] = hid[...]
    small[:n_wt] = jnp.zeros((n_wt,) + small.shape[1:], F32)

    @pl.when(me == 0)
    def _():
        e_in[...] = jnp.zeros_like(e_in)
        prev_b[...] = jnp.zeros_like(prev_b)

    @pl.when(me == count - 1)
    def _():
        next_b[...] = jnp.zeros_like(next_b)

    swap.wait()
    floats = hid_all[...].astype(F32)
    scale = lax.rsqrt(jnp.mean(floats * floats, axis=-1, keepdims=True) + EPS)
    normed[...] = (floats * scale * norm_gain[...]).astype(BF)
    sends = []
    for k in range(1, n_wt):
        sends.append(remote(normed.at[:, block(lax.rem(w + k, n_wt), depth)], rows.at[k],
                            sem_r.at[k], peer(k)))
        sends[-1].start()
    rows[0] = normed[:, block(w, depth)]
    load_x.wait()
    tile = min(512, chan)
    backs = []
    for k in range(n_wt):
        if k:
            sends[k - 1].wait()

        @pl.loop(0, chan // tile)
        def _(i):
            prod[k, :, block(i, tile)] = dot(rows[k], wx[:, block(i, tile)]).astype(BF)

        n_bc = wbc.shape[1]
        small[k, :, :n_bc] = dot(rows[k], wbc[...])
        small[k, :, n_bc:n_bc + heads] = dot(rows[k], wdt[...])
        if k:
            backs.append(remote(small.at[k], small.at[n_wt - 1 + k], sem_s.at[k], peer(-k)))
            backs.append(remote(prod.at[k], prod.at[n_wt - 1 + k], sem_p.at[k], peer(-k)))
            backs[-2].start()
            backs[-1].start()
    s_sum = small[0]
    for k in range(1, n_wt):
        backs[2 * k - 2].wait()
        s_sum = s_sum + small[n_wt - 1 + k]
    n_state = n_bc // 2
    bc = silu(s_sum[:, :n_bc])
    b, c = bc[:, :n_state].astype(BF), bc[:, n_state:].astype(BF)
    t_at = lax.broadcasted_iota(jnp.int32, (tokens, 128), 0)
    raw = s_sum[:, n_bc:] + params[0:1, :]
    soft = jnp.maximum(raw, 0.0) + jnp.log1p(jnp.exp(-jnp.abs(raw)))
    dt = jnp.where(t_at.astype(F32) < params[3:4, :], soft, 0.0)
    log = -dt * jnp.exp(params[1:2, :])
    lower = t_at >= lax.broadcasted_iota(jnp.int32, (tokens, tokens), 1)
    cum = jnp.dot(lower.astype(F32), log, precision=lax.Precision.HIGHEST, preferred_element_type=F32)
    cum_t[...] = cum.T
    dt_t[...] = dt.T
    b_f, c_f = b.astype(F32), c.astype(F32)
    b_t = b_f.T
    scores = dot(c, b_t.astype(BF))
    for k in range(1, n_wt):
        backs[2 * k - 1].wait()

    def head_cols(h):
        return block(h, 128)

    @pl.loop(0, heads)
    def _(h):
        at = head_cols(h)
        total = prod[0, :, at].astype(F32)
        for k in range(1, n_wt):
            total = total + prod[n_wt - 1 + k, :, at].astype(F32)
        x_h = silu(total).astype(BF)
        x_in[:, at] = x_h
        row = cum_t[pl.ds(h, 1), :]
        tail = jnp.exp(row[:, tokens - 1:] - row) * dt_t[pl.ds(h, 1), :]
        fresh[h] = dot((b_t * tail).astype(BF), x_h)

    def state_copy(h):
        return remote(e_out.at[h], e_in.at[h], sem_e.at[h], shard(1))

    def y_copy(h, k):
        at = head_cols(h)
        return remote(yb.at[0, :, at], yb.at[k, :, at], sem_y.at[h, k], peer(k))

    @pl.loop(0, heads)
    def _(h):
        at = head_cols(h)
        row = cum_t[pl.ds(h, 1), :]
        wide = jnp.broadcast_to(row, (tokens, tokens))
        tall = wide.T
        decay = jnp.exp(jnp.where(lower, tall - wide, -jnp.inf))
        x_h = x_in[:, at]
        y = dot((scores * decay * dt_t[pl.ds(h, 1), :]).astype(BF), x_h)
        y = y + gains[1:2, at] * x_h.astype(F32)
        grown = (c_f * jnp.exp(tall)).astype(BF)

        @pl.when(me > 0)
        def _():
            state_copy(h).wait_recv()

        entering = e_in[h]

        @pl.when(me < count - 1)
        def _():
            e_out[h] = (jnp.exp(row[:, tokens - 1:]) * entering.astype(F32) + fresh[h]).astype(BF)
            state_copy(h).start()

        y = y + dot(grown, entering)
        scaling = lax.rsqrt(jnp.mean(y * y, axis=-1, keepdims=True) + EPS)
        yb[0, :, at] = (y * scaling * gains[0:1, at]).astype(BF)
        for k in range(1, n_wt):
            y_copy(h, k).start()

    @pl.when(me < count - 1)
    def _():
        @pl.loop(0, heads)
        def _(h):
            state_copy(h).wait_send()

    load_o.wait()
    o_tile = min(256, cols)
    o_copies = []
    for k in range(n_wt):
        if k:
            @pl.loop(0, heads)
            def _(h):
                y_copy(h, k).wait()

        @pl.loop(0, cols // o_tile)
        def _(i):
            po[k, :, block(i, o_tile)] = dot(yb[k], wo[:, block(i, o_tile)]).astype(BF)

        if k:
            o_copies.append(remote(po.at[k], partial.at[:, block(w, cols)], sem_o.at[k], peer(-k)))
            o_copies[-1].start()
        else:
            partial[:, block(w, cols)] = po[0]
    for copy in o_copies:
        copy.wait()
    give = remote(partial.at[:, block(1 - hd, half)], hrec, sem_g, sib)
    give.start()
    base = hid[...].astype(F32) + partial[:, block(hd, half)].astype(F32)
    give.wait()
    mixed[...] = (base + hrec[...].astype(F32)).astype(BF)
    up = remote(mixed, prev_b, sem_n.at[0], shard(1))
    down = remote(mixed, next_b, sem_n.at[1], shard(-1))

    @pl.when(me < count - 1)
    def _():
        up.start()

    @pl.when(me > 0)
    def _():
        down.start()

    own = mixed[...].astype(F32) * params[5:6, 0:1]

    @pl.when(me > 0)
    def _():
        up.wait_recv()
        down.wait_send()

    @pl.when(me < count - 1)
    def _():
        down.wait_recv()
        up.wait_send()

    out[...] = (own + params[4:5, 0:1] * prev_b[...].astype(F32)
                + params[6:7, 0:1] * next_b[...].astype(F32)).astype(BF)


def body(hidden, norm_gain, w_x, w_bc, w_dt, dt_bias, a_log, d_skip, inner_gain, w_out,
         lengths, mix_index, mix_gain):
    tokens, half = hidden.shape
    width = norm_gain.shape[0]
    depth, chan = w_x.shape
    heads = w_dt.shape[1]
    size = chan // heads
    n_seq, n_wt = lax.axis_size("seq"), lax.axis_size("wt")
    cols = w_out.shape[1]
    rel = mix_index[0] - lax.axis_index(("seq", "wt"))
    mix = [jnp.sum(jnp.where(rel == j, mix_gain[0], 0.0)) for j in (-1, 0, 1)]
    pad = lambda v: jnp.pad(v, (0, 128 - heads))
    fill = lambda v: jnp.full((128,), v, F32)
    params = jnp.stack([pad(dt_bias), pad(a_log), fill(0.0), fill(lengths[0].astype(F32)),
                        fill(mix[0]), fill(1.0 + mix[1]), fill(mix[2]), fill(0.0)])
    gains = jnp.stack([inner_gain, jnp.repeat(d_skip, size)])
    slots = 2 * n_wt - 1
    vm, anyw = pl.BlockSpec(memory_space=pltpu.VMEM), pl.BlockSpec(memory_space=pl.ANY)
    V = pltpu.VMEM
    n_small = w_bc.shape[1] + 128
    return pl.pallas_call(
        functools.partial(kernel, n_seq, n_wt, heads),
        out_shape=jax.ShapeDtypeStruct((tokens, half), BF),
        in_specs=[vm, vm, vm, vm, anyw, vm, vm, anyw],
        out_specs=vm,
        scratch_shapes=[
            V((tokens, width), BF), V((tokens, width), BF), V((n_wt, tokens, depth), BF),
            V((slots, tokens, chan), BF), V((slots, tokens, n_small), F32),
            V((depth, chan), BF), V((chan, cols), BF), V((tokens, chan), BF),
            V((128, tokens), F32), V((128, tokens), F32), V((heads, size, size), F32),
            V((heads, size, size), BF), V((heads, size, size), BF), V((n_wt, tokens, chan), BF),
            V((n_wt, tokens, cols), BF), V((tokens, width), BF), V((tokens, half), BF),
            V((tokens, half), BF), V((tokens, half), BF), V((tokens, half), BF),
            DMA((2,)), DMA((2,)), DMA((n_wt, 2)), DMA((n_wt, 2)), DMA((n_wt, 2)), DMA((heads, 2)),
            DMA((heads, n_wt, 2)), DMA((n_wt, 2)), DMA((2,)), DMA((2, 2)),
        ],
        compiler_params=pltpu.CompilerParams(
            collective_id=0, has_side_effects=True, vmem_limit_bytes=48 * 2**20
        ),
    )(hidden, params, norm_gain[None, :], gains, w_x, w_bc, w_dt, w_out)


def solution(mesh):
    in_specs = (
        P(("grp", "seq", "wt"), "head"), P(), P("wt", "head"), P("wt", "head"), P("wt", "head"),
        P("head"), P("head"), P("head"), P("head"), P("head", "wt"),
        P(("grp", "seq", "wt")), P(("grp", "seq", "wt"), None), P(("grp", "seq", "wt"), None),
    )
    return jax.shard_map(
        body, mesh=mesh, in_specs=in_specs, out_specs=P(("grp", "seq", "wt"), "head"), check_vma=False
    )
```

time: 147 us -> 116 us (0.79); the launches traced: 144 us -> 115 us
  Pallas kernels: 0 us -> 103 us
  waiting for transfers between devices: 89.5 us -> 0 us
  starting transfers between devices: 35.9 us -> 0 us
  local copies, waits for them, and re-layouts: 1.74 us -> 9.28 us
  matrix products: 6.99 us -> 0 us
  other arithmetic: 6.13 us -> 2.08 us
  blocking collectives: 2.51 us -> 0 us
    pallas_call x0 -> x1, Pallas kernels: none -> 103 us  [body(): pl.pallas_call(functools.partial(kernel, n_seq, n_wt, heads), out_shape=j...]
    ppermute x15 -> x0, waiting for transfers between devices: 89.5 us -> none  [the longest x2 19.1 us: body(): lax.ppermute(decay_sum, ('seq', 'wt'), [(i, i + span) for i in range(coun...]
    ppermute x15 -> x0, starting transfers between devices: 35.9 us -> none  [the longest x3 8.3 us: body(): lax.ppermute(entering.astype(BF), ('seq', 'wt'), [(i, i + span) for i in...]
    dot_general x8 -> x0, matrix products: 6.7 us -> none  [the longest x5 5.52 us: dot(): return jnp.dot(a, b, preferred_element_type=F32)]
    unnamed x18 -> x10, local copies, waits for them, and re-layouts: 0.04 us -> 6.5 us
    convert_element_type x10 -> x0, other arithmetic: 5.13 us -> none  [the longest x1 2.05 us: body(): return out.astype(BF)]
    all_gather x1 -> x0, blocking collectives: 2.51 us -> none  [body(): whole = lax.all_gather(hidden, 'head', axis=1, tiled=True)]
    another operation x0 -> x7, local copies, waits for them, and re-layouts: none -> 2.06 us  [the longest x6 2.05 us: body(): jnp.stack([pad(dt_bias), pad(a_log), fill(0.0), fill(lengths[0].astype(F3...]
  transfers between devices with their start and end apart: 15 -> 0, of which waited for: 12 -> 0; matrix products, arithmetic and copies ran while one was open for 2% -> 0% of each run, Pallas kernels for 0% -> 0%
where the time goes in v3:
time: 116 us; the launch traced here: 115 us
  Pallas kernels  103 us (89%)
  local copies, waits for them, and re-layouts  9.28 us (8%)
  other arithmetic  2.08 us (2%)
  between operations  1.28 us (1%)
    pallas_call x1, Pallas kernels, body(): pl.pallas_call(functools.partial(kernel, n_seq, n_wt, heads), out_shape=j...  103 us
    unnamed x10, local copies, waits for them, and re-layouts  6.5 us

profile of v3, /device:TPU:22, one launch (start us, length us, event | category | flops | bytes accessed | tf_op | source)
XLA Modules:
  0.0 115.5 jit_solution(7120298768994006306)
XLA Ops:
  0.7 1.4 %fusion.2 = (f32[]{:T(128)}, f32[]{:T(128)}, f32[]{:T(128)}) fusion(f32[1,4]{1,0:T(1,128)} %param.25, s32[1,4]{1,0:T(1,128)} %param.24, s32[]{:T(128)S(6)} %add.7), kind=kLoop, calls=%fused_computation.6 | loop fusion | flops 37 | bytes 48 | tf_op jit(solution)/shard_map/reduce_sum | solution.py:244
  2.6 0.6 stack_broadcast_in_dim.15
  3.3 0.7 stack_broadcast_in_dim.13
  4.0 0.7 pad_bitcast_fusion
  4.7 0.7 broadcast_in_dim.14
  5.4 0.7 pad_maximum_fusion.gains
  6.1 0.9 copy.14.wdt
  7.0 0.0 copy-start
  7.1 2.2 %copy-done = bf16[1024,2048]{1,0:T(8,128)(2,1)S(1)} copy-done((bf16[1024,2048]{1,0:T(8,128)(2,1)S(1)}, bf16[1024,2048]{1,0:T(8,128)(2,1)}, u32[]{:S(2)}) %copy-start) | copy-done | bytes 4194328
  9.2 0.0 copy-start.1
  9.2 1.0 copy-done.1
  10.3 0.0 copy-start.2
  10.3 0.9 copy-done.2
  11.2 0.0 copy-start.3
  11.2 0.7 copy-done.3
  11.9 102.8 %shard_map.127 = bf16[128,1024]{1,0:T(8,128)(2,1)S(1)} custom-call(bf16[128,1024]{1,0:T(8,128)(2,1)S(1)} %copy-done.2, f32[8,128]{1,0:T(8,128)S(1)} %stack.17.params, f32[1,2048]{1,0:T(1,128)S(1)} %bitcast.8, f32[2,2048]{1,0:T(2,128)S(1)} %pad_maximum_fusion.gains, bf16[1024,2048]{1,0:T(8,128)(2,1)S(1)} %copy-done, bf16[1024,256]{1,0:T(8,128)(2,1)S(1)} %copy-done.1, ...), custom_call_target="tpu_custom_call" | custom-call | tf_op jit(solution)/shard_map/pallas_call | solution.py:254
  114.8 0.7 copy.17
  (4 shorter events, 0.0 us)
Async XLA Ops:
  7.0 2.2 %copy-start = (bf16[1024,2048]{1,0:T(8,128)(2,1)S(1)}, bf16[1024,2048]{1,0:T(8,128)(2,1)}, u32[]{:S(2)}) copy-start(bf16[1024,2048]{1,0:T(8,128)(2,1)} %wx_hbm.1) | copy-start | bytes 12582916
  9.2 1.0 copy-start.1
  10.3 0.9 copy-start.2
  11.2 0.7 copy-start.3

commit v4 on v3

--- a/solution.py
+++ b/solution.py
@@ -22,8 +22,9 @@
     return v * jax.nn.sigmoid(v)
 
 
-def kernel(n_seq, n_wt, heads, hid, params, norm_gain, gains, wx_hbm, wbc, wdt, wo_hbm, out,
-           hid_all, normed, rows, prod, small, wx, wo, x_in, cum_t, dt_t, fresh, e_in, e_out, yb,
+def kernel(n_seq, n_wt, heads, hid_hbm, dt_bias, a_log, d_skip, lengths, mix_index, mix_gain, norm_gain,
+           inner_gain, wx_hbm, wbc_hbm, wdt, wo_hbm, out, hid, wbc, params, y_loc, grow,
+           hid_all, normed, rows, prod, small, wx, wo, cum_t, dt_t, fresh, e_in, e_out, yb,
            po, partial, hrec, mixed, prev_b, next_b,
            sem_w, sem_h, sem_r, sem_p, sem_s, sem_e, sem_y, sem_o, sem_g, sem_n):
     z, w, hd = lax.axis_index("seq"), lax.axis_index("wt"), lax.axis_index("head")
@@ -47,8 +48,17 @@
 
     load_x = pltpu.make_async_copy(wx_hbm, wx, sem_w.at[0])
     load_o = pltpu.make_async_copy(wo_hbm, wo, sem_w.at[1])
+    load_h = pltpu.make_async_copy(hid_hbm, hid, sem_w.at[2])
+    load_b = pltpu.make_async_copy(wbc_hbm, wbc, sem_w.at[3])
+    load_h.start()
+    load_b.start()
     load_x.start()
     load_o.start()
+    params[...] = jnp.zeros_like(params)
+    params[0:1, :heads] = dt_bias[...]
+    params[1:2, :heads] = a_log[...]
+    rel = [mix_index[0, k] - me for k in range(mix_index.shape[1])]
+    mix = [sum(jnp.where(r == j, mix_gain[0, k], 0.0) for k, r in enumerate(rel)) for j in (-1, 0, 1)]
     barrier = pltpu.get_barrier_semaphore()
     for device in [sib, shard(1), shard(-1)] + [peer(k) for k in range(1, n_wt)]:
         pl.semaphore_signal(barrier, inc=1, device_id=device, device_id_type=MESH)
@@ -58,6 +68,7 @@
         return pl.ds(pl.multiple_of(at * size, 128), size)
 
     swap = remote(hid, hid_all.at[:, block(hd, half)], sem_h, sib)
+    load_h.wait()
     swap.start()
     hid_all[:, block(hd, half)] = hid[...]
     small[:n_wt] = jnp.zeros((n_wt,) + small.shape[1:], F32)
@@ -81,28 +92,37 @@
                             sem_r.at[k], peer(k)))
         sends[-1].start()
     rows[0] = normed[:, block(w, depth)]
+    load_b.wait()
     load_x.wait()
     tile = min(512, chan)
+    tiles = chan // tile
     backs = []
+
+    def prod_copy(k, i):
+        return remote(prod.at[k, :, block(i, tile)], prod.at[n_wt - 1 + k, :, block(i, tile)],
+                      sem_p.at[k, i], peer(-k))
+
     for k in range(n_wt):
         if k:
             sends[k - 1].wait()
 
-        @pl.loop(0, chan // tile)
+        n_bc = wbc.shape[1]
+        small[k, :, :n_bc] = dot(rows[k], wbc[...])
+        small[k, :, n_bc:n_bc + heads] = lax.dot_general(
+            rows[k], wdt[...], (((1,), (1,)), ((), ())), preferred_element_type=F32)
+        if k:
+            backs.append(remote(small.at[k], small.at[n_wt - 1 + k], sem_s.at[k], peer(-k)))
+            backs[-1].start()
+
+        @pl.loop(0, tiles)
         def _(i):
             prod[k, :, block(i, tile)] = dot(rows[k], wx[:, block(i, tile)]).astype(BF)
-
-        n_bc = wbc.shape[1]
-        small[k, :, :n_bc] = dot(rows[k], wbc[...])
-        small[k, :, n_bc:n_bc + heads] = dot(rows[k], wdt[...])
-        if k:
-            backs.append(remote(small.at[k], small.at[n_wt - 1 + k], sem_s.at[k], peer(-k)))
-            backs.append(remote(prod.at[k], prod.at[n_wt - 1 + k], sem_p.at[k], peer(-k)))
-            backs[-2].start()
-            backs[-1].start()
+            if k:
+                prod_copy(k, i).start()
+
     s_sum = small[0]
     for k in range(1, n_wt):
-        backs[2 * k - 2].wait()
+        backs[k - 1].wait()
         s_sum = s_sum + small[n_wt - 1 + k]
     n_state = n_bc // 2
     bc = silu(s_sum[:, :n_bc])
@@ -110,7 +130,7 @@
     t_at = lax.broadcasted_iota(jnp.int32, (tokens, 128), 0)
     raw = s_sum[:, n_bc:] + params[0:1, :]
     soft = jnp.maximum(raw, 0.0) + jnp.log1p(jnp.exp(-jnp.abs(raw)))
-    dt = jnp.where(t_at.astype(F32) < params[3:4, :], soft, 0.0)
+    dt = jnp.where(t_at < lengths[0], soft, 0.0)
     log = -dt * jnp.exp(params[1:2, :])
     lower = t_at >= lax.broadcasted_iota(jnp.int32, (tokens, tokens), 1)
     cum = jnp.dot(lower.astype(F32), log, precision=lax.Precision.HIGHEST, preferred_element_type=F32)
@@ -119,23 +139,35 @@
     b_f, c_f = b.astype(F32), c.astype(F32)
     b_t = b_f.T
     scores = dot(c, b_t.astype(BF))
-    for k in range(1, n_wt):
-        backs[2 * k - 1].wait()
 
     def head_cols(h):
         return block(h, 128)
 
-    @pl.loop(0, heads)
-    def _(h):
+    def one_head(h):
         at = head_cols(h)
         total = prod[0, :, at].astype(F32)
         for k in range(1, n_wt):
             total = total + prod[n_wt - 1 + k, :, at].astype(F32)
         x_h = silu(total).astype(BF)
-        x_in[:, at] = x_h
         row = cum_t[pl.ds(h, 1), :]
-        tail = jnp.exp(row[:, tokens - 1:] - row) * dt_t[pl.ds(h, 1), :]
+        dt_row = dt_t[pl.ds(h, 1), :]
+        tail = jnp.exp(row[:, tokens - 1:] - row) * dt_row
         fresh[h] = dot((b_t * tail).astype(BF), x_h)
+        wide = jnp.broadcast_to(row, (tokens, tokens))
+        tall = wide.T
+        decay = jnp.exp(jnp.where(lower, tall - wide, -jnp.inf))
+        y = dot((scores * decay * dt_row).astype(BF), x_h)
+        y_loc[:, at] = y + d_skip[h] * x_h.astype(F32)
+        grow[h] = (c_f * jnp.exp(tall)).astype(BF)
+
+    per_tile = tile // 128
+
+    @pl.loop(0, tiles)
+    def _(i):
+        for k in range(1, n_wt):
+            prod_copy(k, i).wait()
+        for j in range(per_tile):
+            one_head(i * per_tile + j)
 
     def state_copy(h):
         return remote(e_out.at[h], e_in.at[h], sem_e.at[h], shard(1))
@@ -148,14 +180,6 @@
     def _(h):
         at = head_cols(h)
         row = cum_t[pl.ds(h, 1), :]
-        wide = jnp.broadcast_to(row, (tokens, tokens))
-        tall = wide.T
-        decay = jnp.exp(jnp.where(lower, tall - wide, -jnp.inf))
-        x_h = x_in[:, at]
-        y = dot((scores * decay * dt_t[pl.ds(h, 1), :]).astype(BF), x_h)
-        y = y + gains[1:2, at] * x_h.astype(F32)
-        grown = (c_f * jnp.exp(tall)).astype(BF)
-
         @pl.when(me > 0)
         def _():
             state_copy(h).wait_recv()
@@ -167,9 +191,9 @@
             e_out[h] = (jnp.exp(row[:, tokens - 1:]) * entering.astype(F32) + fresh[h]).astype(BF)
             state_copy(h).start()
 
-        y = y + dot(grown, entering)
+        y = y_loc[:, at] + dot(grow[h], entering)
         scaling = lax.rsqrt(jnp.mean(y * y, axis=-1, keepdims=True) + EPS)
-        yb[0, :, at] = (y * scaling * gains[0:1, at]).astype(BF)
+        yb[0, :, at] = (y * scaling * inner_gain[0:1, at]).astype(BF)
         for k in range(1, n_wt):
             y_copy(h, k).start()
 
@@ -215,7 +239,7 @@
     def _():
         down.start()
 
-    own = mixed[...].astype(F32) * params[5:6, 0:1]
+    own = mixed[...].astype(F32) * (1.0 + mix[1])
 
     @pl.when(me > 0)
     def _():
@@ -227,8 +251,8 @@
         down.wait_recv()
         up.wait_send()
 
-    out[...] = (own + params[4:5, 0:1] * prev_b[...].astype(F32)
-                + params[6:7, 0:1] * next_b[...].astype(F32)).astype(BF)
+    out[...] = (own + mix[0] * prev_b[...].astype(F32)
+                + mix[2] * next_b[...].astype(F32)).astype(BF)
 
 
 def body(hidden, norm_gain, w_x, w_bc, w_dt, dt_bias, a_log, d_skip, inner_gain, w_out,
@@ -240,37 +264,33 @@
     size = chan // heads
     n_seq, n_wt = lax.axis_size("seq"), lax.axis_size("wt")
     cols = w_out.shape[1]
-    rel = mix_index[0] - lax.axis_index(("seq", "wt"))
-    mix = [jnp.sum(jnp.where(rel == j, mix_gain[0], 0.0)) for j in (-1, 0, 1)]
-    pad = lambda v: jnp.pad(v, (0, 128 - heads))
-    fill = lambda v: jnp.full((128,), v, F32)
-    params = jnp.stack([pad(dt_bias), pad(a_log), fill(0.0), fill(lengths[0].astype(F32)),
-                        fill(mix[0]), fill(1.0 + mix[1]), fill(mix[2]), fill(0.0)])
-    gains = jnp.stack([inner_gain, jnp.repeat(d_skip, size)])
     slots = 2 * n_wt - 1
     vm, anyw = pl.BlockSpec(memory_space=pltpu.VMEM), pl.BlockSpec(memory_space=pl.ANY)
-    V = pltpu.VMEM
+    V, sm = pltpu.VMEM, pl.BlockSpec(memory_space=pltpu.SMEM)
     n_small = w_bc.shape[1] + 128
     return pl.pallas_call(
         functools.partial(kernel, n_seq, n_wt, heads),
         out_shape=jax.ShapeDtypeStruct((tokens, half), BF),
-        in_specs=[vm, vm, vm, vm, anyw, vm, vm, anyw],
+        in_specs=[anyw, vm, vm, sm, sm, sm, sm, vm, vm, anyw, anyw, vm, anyw],
         out_specs=vm,
         scratch_shapes=[
+            V((tokens, half), BF), V(w_bc.shape, BF), V((8, 128), F32), V((tokens, chan), F32),
+            V((heads, tokens, size), BF),
             V((tokens, width), BF), V((tokens, width), BF), V((n_wt, tokens, depth), BF),
             V((slots, tokens, chan), BF), V((slots, tokens, n_small), F32),
-            V((depth, chan), BF), V((chan, cols), BF), V((tokens, chan), BF),
+            V((depth, chan), BF), V((chan, cols), BF),
             V((128, tokens), F32), V((128, tokens), F32), V((heads, size, size), F32),
             V((heads, size, size), BF), V((heads, size, size), BF), V((n_wt, tokens, chan), BF),
             V((n_wt, tokens, cols), BF), V((tokens, width), BF), V((tokens, half), BF),
             V((tokens, half), BF), V((tokens, half), BF), V((tokens, half), BF),
-            DMA((2,)), DMA((2,)), DMA((n_wt, 2)), DMA((n_wt, 2)), DMA((n_wt, 2)), DMA((heads, 2)),
+            DMA((4,)), DMA((2,)), DMA((n_wt, 2)), DMA((n_wt, chan // 128, 2)), DMA((n_wt, 2)), DMA((heads, 2)),
             DMA((heads, n_wt, 2)), DMA((n_wt, 2)), DMA((2,)), DMA((2, 2)),
         ],
         compiler_params=pltpu.CompilerParams(
-            collective_id=0, has_side_effects=True, vmem_limit_bytes=48 * 2**20
+            collective_id=0, has_side_effects=True, vmem_limit_bytes=63 * 2**20
         ),
-    )(hidden, params, norm_gain[None, :], gains, w_x, w_bc, w_dt, w_out)
+    )(hidden, dt_bias[None, :], a_log[None, :], d_skip, lengths, mix_index, mix_gain, norm_gain[None, :],
+      inner_gain[None, :], w_x, w_bc, w_dt.T, w_out)
 
 
 def solution(mesh):

time: 116 us -> 103 us (0.89)
  local copies, waits for them, and re-layouts: 9.28 us -> 1.67 us
  Pallas kernels: 103 us -> 100 us
  other arithmetic: 2.08 us -> 0 us
    unnamed x10 -> x1, local copies, waits for them, and re-layouts: 6.5 us -> 1.67 us
    pallas_call x1, Pallas kernels: 103 us -> 100 us  [body(): pl.pallas_call(functools.partial(kernel, n_seq, n_wt, heads), out_shape=j...]
    another operation x7 -> x0, local copies, waits for them, and re-layouts: 2.06 us -> none  [the longest x6 2.05 us: body(): jnp.stack([pad(dt_bias), pad(a_log), fill(0.0), fill(lengths[0].astype(F3...]
    reduce_sum x1 -> x0, other arithmetic: 1.37 us -> none  [body(): mix = [jnp.sum(jnp.where(rel == j, mix_gain[0], 0.0)) for j in (-1, 0, 1)]]
where the time goes in v4:
time: 103 us; the launch traced here: 102 us
  Pallas kernels  100 us (97%)
  local copies, waits for them, and re-layouts  1.67 us (2%)
    pallas_call x1, Pallas kernels, body(): pl.pallas_call(functools.partial(kernel, n_seq, n_wt, heads), out_shape=j...  100 us

profile of v4, /device:TPU:22, one launch (start us, length us, event | category | flops | bytes accessed | tf_op | source)
XLA Modules:
  0.0 102.3 jit_solution(18087996820105854782)
XLA Ops:
  0.7 100.0 %shard_map.127 = bf16[128,1024]{1,0:T(8,128)(2,1)} custom-call(bf16[128,1024]{1,0:T(8,128)(2,1)} %hid_hbm.1, f32[1,16]{1,0:T(1,128)} %bitcast.8, f32[1,16]{1,0:T(1,128)} %bitcast.9, f32[16]{0:T(128)} %d_skip.1, s32[1]{0:T(128)S(6)} %copy.15.lengths, s32[1,4]{1,0:T(1,128)} %mix_index.1, f32[1,4]{1,0:T(1,128)} %mix_gain.1, f32[1,2048]{1,0:T(1,128)} %bitcast.6, ...), custom_call_target="tpu_custom_call" | custom-call | tf_op jit(solution)/shard_map/pallas_call | solution.py:271
  100.6 1.7 %copy.16 = bf16[128,1024]{1,0:T(8,128)(2,1)} copy(bf16[128,1024]{1,0:T(8,128)(2,1)} %shard_map.127) | data formatting | bytes 524288

commit v5 on v4

--- a/solution.py
+++ b/solution.py
@@ -24,9 +24,9 @@
 
 def kernel(n_seq, n_wt, heads, hid_hbm, dt_bias, a_log, d_skip, lengths, mix_index, mix_gain, norm_gain,
            inner_gain, wx_hbm, wbc_hbm, wdt, wo_hbm, out, hid, wbc, params, y_loc, grow,
-           hid_all, normed, rows, prod, small, wx, wo, cum_t, dt_t, fresh, e_in, e_out, yb,
+           hid_all, normed, rows, prod, small, bcs, wx, wo, cum_t, dt_t, fresh, e_in, e_out, yb, yh,
            po, partial, hrec, mixed, prev_b, next_b,
-           sem_w, sem_h, sem_r, sem_p, sem_s, sem_e, sem_y, sem_o, sem_g, sem_n):
+           sem_w, sem_h, sem_r, sem_p, sem_s, sem_b, sem_e, sem_y, sem_o, sem_g, sem_n):
     z, w, hd = lax.axis_index("seq"), lax.axis_index("wt"), lax.axis_index("head")
     tokens, half = hid.shape
     depth, cols = wx.shape[0], wo.shape[1]
@@ -94,12 +94,11 @@
     rows[0] = normed[:, block(w, depth)]
     load_b.wait()
     load_x.wait()
-    tile = min(512, chan)
-    tiles = chan // tile
+    tiles, tile = prod.shape[1], prod.shape[3]
     backs = []
 
     def prod_copy(k, i):
-        return remote(prod.at[k, :, block(i, tile)], prod.at[n_wt - 1 + k, :, block(i, tile)],
+        return remote(prod.at[k, i], prod.at[n_wt - 1 + k, i],
                       sem_p.at[k, i], peer(-k))
 
     for k in range(n_wt):
@@ -107,28 +106,32 @@
             sends[k - 1].wait()
 
         n_bc = wbc.shape[1]
-        small[k, :, :n_bc] = dot(rows[k], wbc[...])
-        small[k, :, n_bc:n_bc + heads] = lax.dot_general(
+        bcs[k] = dot(rows[k], wbc[...]).astype(BF)
+        small[k, :, :heads] = lax.dot_general(
             rows[k], wdt[...], (((1,), (1,)), ((), ())), preferred_element_type=F32)
         if k:
             backs.append(remote(small.at[k], small.at[n_wt - 1 + k], sem_s.at[k], peer(-k)))
+            backs.append(remote(bcs.at[k], bcs.at[n_wt - 1 + k], sem_b.at[k], peer(-k)))
+            backs[-2].start()
             backs[-1].start()
 
         @pl.loop(0, tiles)
         def _(i):
-            prod[k, :, block(i, tile)] = dot(rows[k], wx[:, block(i, tile)]).astype(BF)
+            prod[k, i] = dot(rows[k], wx[:, block(i, tile)]).astype(BF)
             if k:
                 prod_copy(k, i).start()
 
-    s_sum = small[0]
+    s_sum, bc_sum = small[0], bcs[0].astype(F32)
     for k in range(1, n_wt):
-        backs[k - 1].wait()
+        backs[2 * k - 2].wait()
+        backs[2 * k - 1].wait()
         s_sum = s_sum + small[n_wt - 1 + k]
+        bc_sum = bc_sum + bcs[n_wt - 1 + k].astype(F32)
     n_state = n_bc // 2
-    bc = silu(s_sum[:, :n_bc])
+    bc = silu(bc_sum)
     b, c = bc[:, :n_state].astype(BF), bc[:, n_state:].astype(BF)
     t_at = lax.broadcasted_iota(jnp.int32, (tokens, 128), 0)
-    raw = s_sum[:, n_bc:] + params[0:1, :]
+    raw = s_sum + params[0:1, :]
     soft = jnp.maximum(raw, 0.0) + jnp.log1p(jnp.exp(-jnp.abs(raw)))
     dt = jnp.where(t_at < lengths[0], soft, 0.0)
     log = -dt * jnp.exp(params[1:2, :])
@@ -143,11 +146,11 @@
     def head_cols(h):
         return block(h, 128)
 
-    def one_head(h):
-        at = head_cols(h)
-        total = prod[0, :, at].astype(F32)
+    def one_head(h, i, j):
+        at, cut = head_cols(h), slice(j * 128, (j + 1) * 128)
+        total = prod[0, i, :, cut].astype(F32)
         for k in range(1, n_wt):
-            total = total + prod[n_wt - 1 + k, :, at].astype(F32)
+            total = total + prod[n_wt - 1 + k, i, :, cut].astype(F32)
         x_h = silu(total).astype(BF)
         row = cum_t[pl.ds(h, 1), :]
         dt_row = dt_t[pl.ds(h, 1), :]
@@ -167,14 +170,13 @@
         for k in range(1, n_wt):
             prod_copy(k, i).wait()
         for j in range(per_tile):
-            one_head(i * per_tile + j)
+            one_head(i * per_tile + j, i, j)
 
     def state_copy(h):
         return remote(e_out.at[h], e_in.at[h], sem_e.at[h], shard(1))
 
     def y_copy(h, k):
-        at = head_cols(h)
-        return remote(yb.at[0, :, at], yb.at[k, :, at], sem_y.at[h, k], peer(k))
+        return remote(yh.at[0, h], yh.at[k, h], sem_y.at[h, k], peer(k))
 
     @pl.loop(0, heads)
     def _(h):
@@ -193,7 +195,9 @@
 
         y = y_loc[:, at] + dot(grow[h], entering)
         scaling = lax.rsqrt(jnp.mean(y * y, axis=-1, keepdims=True) + EPS)
-        yb[0, :, at] = (y * scaling * inner_gain[0:1, at]).astype(BF)
+        y_h = (y * scaling * inner_gain[0:1, at]).astype(BF)
+        yb[0, :, at] = y_h
+        yh[0, h] = y_h
         for k in range(1, n_wt):
             y_copy(h, k).start()
 
@@ -211,6 +215,7 @@
             @pl.loop(0, heads)
             def _(h):
                 y_copy(h, k).wait()
+                yb[k, :, head_cols(h)] = yh[k, h]
 
         @pl.loop(0, cols // o_tile)
         def _(i):
@@ -267,7 +272,7 @@
     slots = 2 * n_wt - 1
     vm, anyw = pl.BlockSpec(memory_space=pltpu.VMEM), pl.BlockSpec(memory_space=pl.ANY)
     V, sm = pltpu.VMEM, pl.BlockSpec(memory_space=pltpu.SMEM)
-    n_small = w_bc.shape[1] + 128
+    tile = min(512, chan)
     return pl.pallas_call(
         functools.partial(kernel, n_seq, n_wt, heads),
         out_shape=jax.ShapeDtypeStruct((tokens, half), BF),
@@ -277,13 +282,15 @@
             V((tokens, half), BF), V(w_bc.shape, BF), V((8, 128), F32), V((tokens, chan), F32),
             V((heads, tokens, size), BF),
             V((tokens, width), BF), V((tokens, width), BF), V((n_wt, tokens, depth), BF),
-            V((slots, tokens, chan), BF), V((slots, tokens, n_small), F32),
+            V((slots, chan // tile, tokens, tile), BF), V((slots, tokens, 128), F32),
+            V((slots, tokens, w_bc.shape[1]), BF),
             V((depth, chan), BF), V((chan, cols), BF),
             V((128, tokens), F32), V((128, tokens), F32), V((heads, size, size), F32),
             V((heads, size, size), BF), V((heads, size, size), BF), V((n_wt, tokens, chan), BF),
+            V((n_wt, heads, tokens, size), BF),
             V((n_wt, tokens, cols), BF), V((tokens, width), BF), V((tokens, half), BF),
             V((tokens, half), BF), V((tokens, half), BF), V((tokens, half), BF),
-            DMA((4,)), DMA((2,)), DMA((n_wt, 2)), DMA((n_wt, chan // 128, 2)), DMA((n_wt, 2)), DMA((heads, 2)),
+            DMA((4,)), DMA((2,)), DMA((n_wt, 2)), DMA((n_wt, chan // 128, 2)), DMA((n_wt, 2)), DMA((n_wt, 2)), DMA((heads, 2)),
             DMA((heads, n_wt, 2)), DMA((n_wt, 2)), DMA((2,)), DMA((2, 2)),
         ],
         compiler_params=pltpu.CompilerParams(

time: 103 us -> 101 us (0.981)
  Pallas kernels: 100 us -> 98.6 us
    pallas_call x1, Pallas kernels: 100 us -> 98.6 us  [body(): pl.pallas_call(functools.partial(kernel, n_seq, n_wt, heads), out_shape=j...]
where the time goes in v5:
time: 101 us
  Pallas kernels  98.6 us (98%)
  local copies, waits for them, and re-layouts  1.67 us (2%)
    pallas_call x1, Pallas kernels, body(): pl.pallas_call(functools.partial(kernel, n_seq, n_wt, heads), out_shape=j...  98.6 us

profile of v5, /device:TPU:22, one launch (start us, length us, event | category | flops | bytes accessed | tf_op | source)
XLA Modules:
  0.0 100.9 jit_solution(16881434994608432914)
XLA Ops:
  0.7 98.6 %shard_map.127 = bf16[128,1024]{1,0:T(8,128)(2,1)} custom-call(bf16[128,1024]{1,0:T(8,128)(2,1)} %hid_hbm.1, f32[1,16]{1,0:T(1,128)} %bitcast.8, f32[1,16]{1,0:T(1,128)} %bitcast.9, f32[16]{0:T(128)} %d_skip.1, s32[1]{0:T(128)S(6)} %copy.15.lengths, s32[1,4]{1,0:T(1,128)} %mix_index.1, f32[1,4]{1,0:T(1,128)} %mix_gain.1, f32[1,2048]{1,0:T(1,128)} %bitcast.6, ...), custom_call_target="tpu_custom_call" | custom-call | tf_op jit(solution)/shard_map/pallas_call | solution.py:276
  99.2 1.7 %copy.16 = bf16[128,1024]{1,0:T(8,128)(2,1)} copy(bf16[128,1024]{1,0:T(8,128)(2,1)} %shard_map.127) | data formatting | bytes 524288

commit v6 on v5

--- a/solution.py
+++ b/solution.py
@@ -165,21 +165,13 @@
 
     per_tile = tile // 128
 
-    @pl.loop(0, tiles)
-    def _(i):
-        for k in range(1, n_wt):
-            prod_copy(k, i).wait()
-        for j in range(per_tile):
-            one_head(i * per_tile + j, i, j)
-
     def state_copy(h):
         return remote(e_out.at[h], e_in.at[h], sem_e.at[h], shard(1))
 
     def y_copy(h, k):
         return remote(yh.at[0, h], yh.at[k, h], sem_y.at[h, k], peer(k))
 
-    @pl.loop(0, heads)
-    def _(h):
+    def chain_head(h):
         at = head_cols(h)
         row = cum_t[pl.ds(h, 1), :]
         @pl.when(me > 0)
@@ -200,6 +192,17 @@
         yh[0, h] = y_h
         for k in range(1, n_wt):
             y_copy(h, k).start()
+
+    @pl.loop(0, tiles)
+    def _(i):
+        for k in range(1, n_wt):
+            prod_copy(k, i).wait()
+        for j in range(per_tile):
+            one_head(i * per_tile + j, i, j)
+
+        @pl.loop(0, per_tile)
+        def _(j):
+            chain_head(i * per_tile + j)
 
     @pl.when(me < count - 1)
     def _():

time: 101 us -> 98.2 us (0.972)
  Pallas kernels: 98.6 us -> 95.7 us
    pallas_call x1, Pallas kernels: 98.6 us -> 95.7 us  [body(): pl.pallas_call(functools.partial(kernel, n_seq, n_wt, heads), out_shape=j...]
where the time goes in v6:
time: 98.2 us; the launch traced here: 98 us
  Pallas kernels  95.7 us (97%)
  local copies, waits for them, and re-layouts  1.67 us (2%)
    pallas_call x1, Pallas kernels, body(): pl.pallas_call(functools.partial(kernel, n_seq, n_wt, heads), out_shape=j...  95.7 us

profile of v6, /device:TPU:22, one launch (start us, length us, event | category | flops | bytes accessed | tf_op | source)
XLA Modules:
  0.0 98.0 jit_solution(14832616030274594160)
XLA Ops:
  0.7 95.7 %shard_map.127 = bf16[128,1024]{1,0:T(8,128)(2,1)} custom-call(bf16[128,1024]{1,0:T(8,128)(2,1)} %hid_hbm.1, f32[1,16]{1,0:T(1,128)} %bitcast.8, f32[1,16]{1,0:T(1,128)} %bitcast.9, f32[16]{0:T(128)} %d_skip.1, s32[1]{0:T(128)S(6)} %copy.15.lengths, s32[1,4]{1,0:T(1,128)} %mix_index.1, f32[1,4]{1,0:T(1,128)} %mix_gain.1, f32[1,2048]{1,0:T(1,128)} %bitcast.6, ...), custom_call_target="tpu_custom_call" | custom-call | tf_op jit(solution)/shard_map/pallas_call | solution.py:279
  96.3 1.7 %copy.16 = bf16[128,1024]{1,0:T(8,128)(2,1)} copy(bf16[128,1024]{1,0:T(8,128)(2,1)} %shard_map.127) | data formatting | bytes 524288
